TPU v7x, 32 devices: a whole 2x2x4 slice. The times are simulated.
32 devices in a mesh: seq: 8 (over z, x), slot: 4 (over y, core).
Axes of the slice: x: 2, y: 2, z: 4, core: 2. Of those that a mesh axis runs over, the one named last changes fastest.
Arguments:
- hidden_in: bfloat16 [16, 1024, 768], P('slot', 'seq'), may hold values from -6 to 6
- lengths: int32 [16], P('slot'), may hold values from 64 to 1024, as said below
- out_grad: bfloat16 [16, 1024, 768], P('slot', 'seq'), may hold values from -6 to 6
- ln1_gain: bfloat16 [768], replicated, may hold values from 0.25 to 1.75
- ln1_bias: bfloat16 [768], replicated, may hold values from -1.75 to 1.75
- ln2_gain: bfloat16 [768], replicated, may hold values from 0.25 to 1.75
- ln2_bias: bfloat16 [768], replicated, may hold values from -1.75 to 1.75
- w_query: bfloat16 [768, 768], replicated, may hold values from -0.21875 to 0.21875
- b_query: bfloat16 [768], replicated, may hold values from -3 to 3
- w_keyval: bfloat16 [768, 128], replicated, may hold values from -0.21875 to 0.21875
- b_keyval: bfloat16 [128], replicated, may hold values from -3 to 3
- w_out: bfloat16 [768, 768], replicated, may hold values from -3 to 3
- b_out: bfloat16 [768], replicated, may hold values from -3 to 3
- w_up: bfloat16 [768, 3072], replicated, may hold values from -0.21875 to 0.21875
- b_up: bfloat16 [3072], replicated, may hold values from -3 to 3
- w_down: bfloat16 [3072, 768], replicated, may hold values from -0.109375 to 0.109375
- b_down: bfloat16 [768], replicated, may hold values from -3 to 3
Outputs:
- layer_out: bfloat16 [16, 1024, 768], P('slot', 'seq')
- grad_input: float32 [16, 1024, 768], P('slot', 'seq')
- grad_ln1_gain: float32 [768], replicated
- grad_ln1_bias: float32 [768], replicated
- grad_ln2_gain: float32 [768], replicated
- grad_ln2_bias: float32 [768], replicated
- grad_w_query: float32 [768, 768], P('seq', 'slot')
- grad_b_query: float32 [768], replicated
- grad_w_keyval: float32 [768, 128], P('seq', 'slot')
- grad_b_keyval: float32 [128], replicated
- grad_w_out: float32 [768, 768], P('seq', 'slot')
- grad_b_out: float32 [768], replicated
- grad_w_up: float32 [768, 3072], P('seq', 'slot')
- grad_b_up: float32 [3072], replicated
- grad_w_down: float32 [3072, 768], P('seq', 'slot')
- grad_b_down: float32 [768], replicated
Inputs may be any that keep to these rules, and one draw needn't show every extreme that they name: `lengths`: true length of each slot. Of the 4 consecutive slots that share an index of slot, one has length exactly 1024.
All inputs are finite; a program needn't handle non-finite values.
Results may differ from a plain program's by a relative error of at most 0.011.
Values may be sent and summed in bfloat16 or wider, within the bound.
A program may use at most 128 MiB of HBM per device.

v0:
```python
import jax
import jax.numpy as jnp
from jax import lax
from jax.sharding import PartitionSpec as P

HEAD = 64
ROT = 16


def norm(value, gain, bias):
    center = value - jnp.mean(value, axis=-1, keepdims=True)
    spread = jnp.mean(center * center, axis=-1, keepdims=True)
    return center * lax.rsqrt(spread + 1e-05) * gain + bias


def angles(positions):
    half = ROT // 2
    inverse = 10000.0 ** (-(jnp.arange(half, dtype=jnp.float32) * 2.0 / ROT))
    turns = positions[:, None] * inverse[None, :]
    turns = jnp.concatenate([turns, turns], axis=-1)
    return (jnp.cos(turns), jnp.sin(turns))


def turn(value, cosine, sine):
    half = ROT // 2
    part = value[..., :ROT]
    swapped = jnp.concatenate([-part[..., half:], part[..., :half]], axis=-1)
    return jnp.concatenate([part * cosine + swapped * sine, value[..., ROT:]], axis=-1)


def exact_gelu(value):
    return jax.nn.gelu(value, approximate=False)


def body(
    hidden_in,
    lengths,
    out_grad,
    ln1_gain,
    ln1_bias,
    ln2_gain,
    ln2_bias,
    w_query,
    b_query,
    w_keyval,
    b_keyval,
    w_out,
    b_out,
    w_up,
    b_up,
    w_down,
    b_down,
):
    slots_here, span_len, width = hidden_in.shape
    heads = width // HEAD
    total_len = span_len * lax.axis_size("seq")
    scale = HEAD ** (-0.5)
    positions = lax.axis_index("seq") * span_len + jnp.arange(span_len, dtype=jnp.int32)
    key_ids = jnp.arange(total_len, dtype=jnp.int32)
    valid = (positions[None, :] < lengths[:, None]).astype(jnp.float32)[..., None]
    cosine, sine = angles(positions.astype(jnp.float32))
    hidden = hidden_in.astype(jnp.float32)
    attn_in32, norm_one_back = jax.vjp(
        norm, hidden, ln1_gain.astype(jnp.float32), ln1_bias.astype(jnp.float32)
    )
    mlp_in32, norm_two_back = jax.vjp(
        norm, hidden, ln2_gain.astype(jnp.float32), ln2_bias.astype(jnp.float32)
    )
    attn_in = attn_in32.astype(jnp.bfloat16)
    mlp_in = mlp_in32.astype(jnp.bfloat16)
    q_pre = jnp.dot(attn_in, w_query, preferred_element_type=jnp.float32) + b_query.astype(
        jnp.float32
    )
    q_pre = q_pre.reshape(slots_here, span_len, heads, HEAD)
    q_turned, query_back = jax.vjp(lambda v: turn(v, cosine[:, None, :], sine[:, None, :]), q_pre)
    queries = q_turned.astype(jnp.bfloat16)
    kv_pre = jnp.dot(attn_in, w_keyval, preferred_element_type=jnp.float32) + b_keyval.astype(
        jnp.float32
    )
    key_turned, key_back = jax.vjp(lambda v: turn(v, cosine, sine), kv_pre[..., :HEAD])
    kv_local = jnp.concatenate([key_turned, kv_pre[..., HEAD:]], axis=-1).astype(jnp.bfloat16)
    kv_whole = lax.all_gather(kv_local, "seq", axis=1, tiled=True)
    up_pre = jnp.dot(mlp_in, w_up, preferred_element_type=jnp.float32) + b_up.astype(jnp.float32)
    act32, gelu_back = jax.vjp(exact_gelu, up_pre)
    act = act32.astype(jnp.bfloat16)
    mlp_out = jnp.dot(act, w_down, preferred_element_type=jnp.float32) + b_down.astype(jnp.float32)

    def scores_of(query_slot, kv_slot, length):
        raw = (
            jnp.einsum(
                "chd,kd->hck", query_slot, kv_slot[:, :HEAD], preferred_element_type=jnp.float32
            )
            * scale
        )
        allowed = (key_ids[None, :] <= positions[:, None]) & (key_ids[None, :] < length)
        return jnp.where(allowed[None], raw, -1000000000.0)

    def forward_slot(item):
        query_slot, kv_slot, length = item
        scores = scores_of(query_slot, kv_slot, length)
        top = jnp.max(scores, axis=-1, keepdims=True)
        weights = jnp.exp(scores - top)
        summed = jnp.sum(weights, axis=-1, keepdims=True)
        probs = (weights / summed).astype(jnp.bfloat16)
        mixed = jnp.einsum(
            "hck,kd->chd", probs, kv_slot[:, HEAD:], preferred_element_type=jnp.float32
        )
        return (mixed.reshape(span_len, width).astype(jnp.bfloat16), top + jnp.log(summed))

    attn, log_totals = lax.map(forward_slot, (queries, kv_whole, lengths))
    attn_out = jnp.dot(attn, w_out, preferred_element_type=jnp.float32) + b_out.astype(jnp.float32)
    layer_out = (valid * (hidden + attn_out + mlp_out)).astype(jnp.bfloat16)
    grad_low = (out_grad.astype(jnp.float32) * valid).astype(jnp.bfloat16)
    grad_full = grad_low.astype(jnp.float32)
    grad_bias_out = jnp.sum(grad_full, axis=(0, 1))
    grad_w_out = jnp.einsum("std,ste->de", attn, grad_low, preferred_element_type=jnp.float32)
    d_attn = jnp.dot(grad_low, w_out.T, preferred_element_type=jnp.float32).astype(jnp.bfloat16)
    grad_w_down = jnp.einsum("stf,ste->fe", act, grad_low, preferred_element_type=jnp.float32)
    d_act = jnp.dot(grad_low, w_down.T, preferred_element_type=jnp.float32)
    d_up = gelu_back(d_act)[0].astype(jnp.bfloat16)
    grad_b_up = jnp.sum(d_up.astype(jnp.float32), axis=(0, 1))
    grad_w_up = jnp.einsum("std,stf->df", mlp_in, d_up, preferred_element_type=jnp.float32)
    d_mlp_in = jnp.dot(d_up, w_up.T, preferred_element_type=jnp.float32)

    def backward_slot(item):
        query_slot, kv_slot, length, log_total, d_slot = item
        scores = scores_of(query_slot, kv_slot, length)
        probs = jnp.exp(scores - log_total)
        d_probs = jnp.einsum(
            "chd,kd->hck", d_slot, kv_slot[:, HEAD:], preferred_element_type=jnp.float32
        )
        d_scores = (probs * (d_probs - jnp.sum(probs * d_probs, axis=-1, keepdims=True))).astype(
            jnp.bfloat16
        )
        d_query = (
            jnp.einsum(
                "hck,kd->chd", d_scores, kv_slot[:, :HEAD], preferred_element_type=jnp.float32
            )
            * scale
        )
        d_key = (
            jnp.einsum("hck,chd->kd", d_scores, query_slot, preferred_element_type=jnp.float32)
            * scale
        )
        d_value = jnp.einsum(
            "hck,chd->kd", probs.astype(jnp.bfloat16), d_slot, preferred_element_type=jnp.float32
        )
        return (d_query, jnp.concatenate([d_key, d_value], axis=-1))

    d_attn_heads = d_attn.reshape(slots_here, span_len, heads, HEAD)
    d_query, d_kv_terms = lax.map(
        backward_slot, (queries, kv_whole, lengths, log_totals, d_attn_heads)
    )
    d_kv = lax.psum_scatter(d_kv_terms, "seq", scatter_dimension=1, tiled=True)
    d_key_pre = key_back(d_kv[..., :HEAD])[0]
    d_kv_pre = jnp.concatenate([d_key_pre, d_kv[..., HEAD:]], axis=-1).astype(jnp.bfloat16)
    d_q_pre = query_back(d_query)[0].reshape(slots_here, span_len, width).astype(jnp.bfloat16)
    grad_b_query = jnp.sum(d_q_pre.astype(jnp.float32), axis=(0, 1))
    grad_b_keyval = jnp.sum(d_kv_pre.astype(jnp.float32), axis=(0, 1))
    grad_w_query = jnp.einsum("std,ste->de", attn_in, d_q_pre, preferred_element_type=jnp.float32)
    grad_w_keyval = jnp.einsum("std,ste->de", attn_in, d_kv_pre, preferred_element_type=jnp.float32)
    d_attn_in = jnp.dot(d_q_pre, w_query.T, preferred_element_type=jnp.float32) + jnp.dot(
        d_kv_pre, w_keyval.T, preferred_element_type=jnp.float32
    )
    d_hidden_one, grad_gain_one, grad_shift_one = norm_one_back(d_attn_in)
    d_hidden_two, grad_gain_two, grad_shift_two = norm_two_back(d_mlp_in)
    grad_input = grad_full + d_hidden_one + d_hidden_two
    small = lax.psum(
        (
            grad_gain_one,
            grad_shift_one,
            grad_gain_two,
            grad_shift_two,
            grad_b_query,
            grad_b_keyval,
            grad_bias_out,
            grad_b_up,
            grad_bias_out,
        ),
        ("seq", "slot"),
    )
    query_rows, keyval_rows, out_rows, up_rows, down_rows = (
        lax.psum_scatter(grad_w_query, "seq", scatter_dimension=0, tiled=True),
        lax.psum_scatter(grad_w_keyval, "seq", scatter_dimension=0, tiled=True),
        lax.psum_scatter(grad_w_out, "seq", scatter_dimension=0, tiled=True),
        lax.psum_scatter(grad_w_up, "seq", scatter_dimension=0, tiled=True),
        lax.psum_scatter(grad_w_down, "seq", scatter_dimension=0, tiled=True),
    )
    query_part, keyval_part, out_part, up_part, down_part = (
        lax.psum_scatter(query_rows, "slot", scatter_dimension=1, tiled=True),
        lax.psum_scatter(keyval_rows, "slot", scatter_dimension=1, tiled=True),
        lax.psum_scatter(out_rows, "slot", scatter_dimension=1, tiled=True),
        lax.psum_scatter(up_rows, "slot", scatter_dimension=1, tiled=True),
        lax.psum_scatter(down_rows, "slot", scatter_dimension=1, tiled=True),
    )
    return (
        layer_out,
        grad_input,
        small[0],
        small[1],
        small[2],
        small[3],
        query_part,
        small[4],
        keyval_part,
        small[5],
        out_part,
        small[6],
        up_part,
        small[7],
        down_part,
        small[8],
    )


def solution(mesh):
    placed = (
        P("slot", "seq", None),
        P("slot"),
        P("slot", "seq", None),
        P(),
        P(),
        P(),
        P(),
        P(),
        P(),
        P(),
        P(),
        P(),
        P(),
        P(),
        P(),
        P(),
        P(),
    )
    return jax.shard_map(
        body,
        mesh=mesh,
        in_specs=placed,
        out_specs=(
            P("slot", "seq", None),
            P("slot", "seq", None),
            P(),
            P(),
            P(),
            P(),
            P("seq", "slot"),
            P(),
            P("seq", "slot"),
            P(),
            P("seq", "slot"),
            P(),
            P("seq", "slot"),
            P(),
            P("seq", "slot"),
            P(),
        ),
        check_vma=False,
    )
```

profile of v0, /device:TPU:0, one launch (start us, length us, event | category | flops | bytes accessed | tf_op | source)
XLA Modules:
  0.0 891.6 jit_solution(8669537868695289690)
XLA Ops:
  12.3 1.7 convolution_add_fusion.2
  15.1 2.1 convolution_add_fusion.1
  17.2 1.9 copy.77
  21.3 3.2 convolution_convert_fusion
  24.5 2.3 copy.79
  28.8 28.6 %all-gather.2.cloned.1.call-done = bf16[4,1024,128]{1,2,0:T(8,128)(2,1)} async-done(((bf16[4,128,128]{1,2,0:T(8,128)(2,1)}), bf16[4,1024,128]{1,2,0:T(8,128)(2,1)}) %all-gather.2.cloned.1.call-update) | async-done | bytes 1048592 | tf_op jit(solution)/shard_map/all_gather | solution.py:82
  57.3 31.2 %while.28 = (s32[]{:T(128)}, bf16[4,128,768]{1,2,0:T(8,128)(2,1)S(1)}, f32[4,12,128,1]{2,1,3,0:T(8,128)}, bf16[4,1024,128]{1,2,0:T(8,128)(2,1)}, s32[4]{0:T(128)...) while((s32[]{:T(128)}, bf16[4,128,768]{1,2,0:T(8,128)(2,1)S(1)}, ...), condition=%wide.region_5.6_spmd.clone.clone, body=%wide.region_2.5_spmd.clone.clone.sunk | while | flops 421887616 | bytes 21030516 | solution.py:110
  63.5 1.7 fusion.154
  86.8 1.7 fusion.154
  89.4 61.8 %while.29 = (s32[]{:T(128)}, f32[4,128,12,64]{1,3,2,0:T(8,128)}, f32[4,1024,128]{1,2,0:T(8,128)}, bf16[4,1024,128]{1,2,0:T(8,128)(2,1)}, s32[4]{0:T(128)}, /*ind...) while((s32[]{:T(128)}, f32[4,128,12,64]{1,3,2,0:T(8,128)}, ...), condition=%wide.region_8.9_spmd.clone.clone, body=%wide.region_6.8_spmd.clone.clone.sunk | while | flops 1030782592 | bytes 57722648 | solution.py:151
  93.8 2.7 fusion.163
  98.2 2.0 fusion.167
  100.2 2.5 fusion.166
  109.2 2.7 fusion.163
  113.6 2.0 fusion.167
  115.6 2.5 fusion.166
  124.7 2.7 fusion.163
  129.1 2.0 fusion.167
  131.1 2.5 fusion.166
  140.2 2.7 fusion.163
  144.5 2.0 fusion.167
  146.5 2.5 fusion.166
  155.8 2.5 convolution_bitcast_fusion.4
  158.5 9.3 %fusion.92 = (u8[128,3072]{1,0:T(8,128)(4,1)S(1)}, u8[128,3072]{1,0:T(8,128)(4,1)S(1)}, f32[4,128,3072]{2,1,0:T(8,128)}) fusion(f32[3072]{0:T(1024)S(1)} %convert_element_type.128, bf16[768,3072]{1,0:T(8,128)(2,1)} %param.34, bf16[4,128,768]{2,1,0:T(8,128)(2,1)S(1)} %copy-done.2, f32[768]{0:T(1024)S(1)} %convert_element_type.126, ...), kind=kOutput, calls=%fused_computation.137 | convolution fusion | flops 2439512064 | bytes 12605440 | tf_op jit(solution)/shard_map/dot_general | solution.py:83
  167.9 2.4 convolution_bitcast_fusion.3
  170.3 16.8 %multiply_convert_fusion = (bf16[4,128,3072]{2,1,0:T(8,128)(2,1)}, f32[4,128,3072]{2,1,0:T(8,128)}) fusion(f32[4,128,3072]{2,1,0:T(8,128)} %get-tuple-element.339, f32[3072]{0:T(1024)} %copy-done.26, u8[128,3072]{1,0:T(8,128)(4,1)S(1)} %get-tuple-element.264, u8[128,3072]{1,0:T(8,128)(4,1)S(1)} %get-tuple-element.263), kind=kLoop, calls=%fused_computation.78 | loop fusion | flops 111673344 | bytes 16527360 | tf_op jit(solution)/shard_map/convert_element_type | solution.py:85
  187.1 31.6 %reduce-scatter.20.cloned.1.call-done = f32[4,128,128]{1,2,0:T(8,128)} async-done(((f32[4,1024,128]{1,2,0:T(8,128)}), f32[4,128,128]{1,2,0:T(8,128)}) %reduce-scatter.20.cloned.1.call-update) | async-done | bytes 262160 | tf_op jit(solution)/shard_map/reduce_scatter | solution.py:154
  222.8 2.1 convolution_bitcast_fusion.5
  225.0 9.4 %convert_reduce_fusion = (f32[3072]{0:T(1024)}, bf16[4,128,3072]{2,1,0:T(8,128)(2,1)S(1)}) fusion(f32[4,128,3072]{2,1,0:T(8,128)} %get-tuple-element.318, bf16[3072,768]{1,0:T(8,128)(2,1)} %param.36, bf16[4,128,768]{2,1,0:T(8,128)(2,1)S(1)} %copy-done.8, f32[4,128]{1,0:T(4,128)S(1)} %copy-done.30, f32[4,128,3072]{2,1,0:T(8,128)} %get-tuple-element.339, ...), kind=kOutput, calls=%fused_computation.76 | convolution fusion | flops 2443834368 | bytes 21260288 | tf_op jit(solution)/shard_map/dot_general | solution.py:119
  236.0 5.4 convolution_bitcast_fusion.2
  241.8 8.4 convolution_bitcast_fusion.1
  250.3 40.0 %reduce-scatter.22.cloned.1.call-done = f32[96,768]{1,0:T(8,128)} async-done(((f32[768,768]{1,0:T(8,128)}), f32[96,768]{1,0:T(8,128)}) %reduce-scatter.22.cloned.1.call-update) | async-done | bytes 294928 | tf_op jit(solution)/shard_map/reduce_scatter | solution.py:183
  290.3 1.9 copy.105
  292.2 69.5 %reduce-scatter.26.cloned.1.call-done = f32[96,768]{1,0:T(8,128)} async-done(((f32[768,768]{1,0:T(8,128)}), f32[96,768]{1,0:T(8,128)}) %reduce-scatter.26.cloned.1.call-update) | async-done | bytes 294928 | tf_op jit(solution)/shard_map/reduce_scatter | solution.py:185
  361.7 1.9 copy.109
  363.7 62.1 %reduce-scatter.24.cloned.1.call-done = f32[96,128]{1,0:T(8,128)} async-done(((f32[768,128]{1,0:T(8,128)}), f32[96,128]{1,0:T(8,128)}) %reduce-scatter.24.cloned.1.call-update) | async-done | bytes 49168 | tf_op jit(solution)/shard_map/reduce_scatter | solution.py:184
  427.4 164.2 %reduce-scatter.28.cloned.1.call-done = f32[96,3072]{1,0:T(8,128)} async-done(((f32[768,3072]{1,0:T(8,128)}), f32[96,3072]{1,0:T(8,128)}) %reduce-scatter.28.cloned.1.call-update) | async-done | bytes 1179664 | tf_op jit(solution)/shard_map/reduce_scatter | solution.py:186
  591.7 5.9 fusion.62
  597.7 160.2 %reduce-scatter.32.cloned.1.call-done = f32[384,768]{1,0:T(8,128)} async-done(((f32[3072,768]{1,0:T(8,128)}), f32[384,768]{1,0:T(8,128)}) %reduce-scatter.32.cloned.1.call-update) | async-done | bytes 1179664 | tf_op jit(solution)/shard_map/reduce_scatter | solution.py:187
  757.8 2.7 copy.111
  760.6 7.0 fusion.60
  770.2 3.9 fusion.90
  775.2 1.9 fusion.119
  777.2 2.0 fusion.84
  779.2 2.7 convert_reduce_fusion.2
  781.9 41.3 %all-reduce.8 = (f32[768]{0:T(1024)}, f32[768]{0:T(1024)}, f32[768]{0:T(1024)}, f32[768]{0:T(1024)}, f32[768]{0:T(1024)}, /*index=5*/f32[128]{0:T(128)}, f32[768]{0:T(1024)S(1)}, f32[3072]{0:T(1024)}) all-reduce(f32[768]{0:T(1024)} %get-tuple-element.274, ...), channel_id=1, replica_groups=mesh['seq'=8,'slot'=4] {'seq','slot'}, use_global_device_ids=true, to_apply=%region_15.16 | all-reduce | flops 7808 | bytes 62464 | tf_op jit(solution)/shard_map/psum | solution.py:168
  826.4 28.6 %reduce-scatter.30.cloned.1.call-done = f32[96,768]{1,0:T(8,128)} async-done(((f32[96,3072]{1,0:T(8,128)}), f32[96,768]{1,0:T(8,128)}) %reduce-scatter.30.cloned.1.call-update) | async-done | bytes 294928 | tf_op jit(solution)/shard_map/reduce_scatter | solution.py:193
  855.0 28.7 %reduce-scatter.40.cloned.1.call-done = f32[192,384]{1,0:T(8,128)} async-done(((f32[768,384]{1,0:T(8,128)}), f32[192,384]{1,0:T(8,128)}) %reduce-scatter.40.cloned.1.call-update) | async-done | bytes 294928
  (262 shorter events, 91.4 us)
Async XLA Ops:
  7.2 7.9 copy-start
  7.2 7.9 copy-start.1
  7.2 7.8 copy-start.38
  7.2 50.1 %all-gather.2.cloned.1.call-start = ((), (), s32[]{:S(2)}) async-start(), calls=%async_computation.11 | async-start | bytes 1179648 | tf_op jit(solution)/shard_map/all_gather | solution.py:82
  10.2 3.8 copy-start.32
  10.2 144.6 %copy-start.21 = (f32[4,128]{1,0:T(4,128)}, f32[4,128]{1,0:T(4,128)S(1)}, u32[]{:S(2)}) copy-start(f32[4,128]{1,0:T(4,128)S(1)} %fusion.110) | copy-start | bytes 6148
  10.9 4.1 copy-start.23
  11.6 3.4 copy-start.35
  15.0 203.8 %reduce-scatter.20.cloned.1.call-start = ((), (), s32[]{:S(2)}) async-start(), calls=%async_computation.12 | async-start | bytes 2359296 | tf_op jit(solution)/shard_map/reduce_scatter | solution.py:154
  102.6 2.3 copy-start.4
  118.1 2.3 copy-start.4
  133.5 2.3 copy-start.4
  135.8 2.2 copy-start.3
  149.0 2.3 copy-start.4
  151.3 139.0 %reduce-scatter.22.cloned.1.call-start = ((), (), s32[]{:S(2)}) async-start(), calls=%async_computation.13 | async-start | bytes 2654208 | tf_op jit(solution)/shard_map/reduce_scatter | solution.py:183
  153.1 2.7 copy-start.2
  153.1 2.7 copy-start.24
  153.1 2.7 copy-start.36
  155.8 2.6 copy-start.39
  155.8 2.7 copy-start.34
  155.8 2.7 copy-start.40
  158.3 203.4 %reduce-scatter.26.cloned.1.call-start = ((), (), s32[]{:S(2)}) async-start(), calls=%async_computation.15 | async-start | bytes 2654208 | tf_op jit(solution)/shard_map/reduce_scatter | solution.py:185
  158.4 9.4 %copy-start.26 = (f32[3072]{0:T(1024)}, f32[3072]{0:T(1024)S(1)}, u32[]{:S(2)}) copy-start(f32[3072]{0:T(1024)S(1)} %convert_element_type.128) | copy-start | bytes 36868
  158.5 9.4 %copy-start.18 = (f32[768]{0:T(1024)}, f32[768]{0:T(1024)S(1)}, u32[]{:S(2)}) copy-start(f32[768]{0:T(1024)S(1)} %convert_element_type.126) | copy-start | bytes 9220
  158.5 9.4 %copy-start.6 = (bf16[4,128,768]{1,2,0:T(8,128)(2,1)S(1)}, bf16[4,128,768]{1,2,0:T(8,128)(2,1)}, u32[]{:S(2)}) copy-start(bf16[4,128,768]{1,2,0:T(8,128)(2,1)} %copy-done.5) | copy-start | bytes 2359300
  158.5 9.4 %copy-start.8 = (bf16[4,128,768]{2,1,0:T(8,128)(2,1)S(1)}, bf16[4,128,768]{2,1,0:T(8,128)(2,1)}, u32[]{:S(2)}) copy-start(bf16[4,128,768]{2,1,0:T(8,128)(2,1)} %param.23) | copy-start | bytes 2359300
  158.5 9.3 %copy-start.29 = (f32[4,128]{1,0:T(4,128)S(1)}, f32[4,128]{1,0:T(4,128)}, u32[]{:S(2)}) copy-start(f32[4,128]{1,0:T(4,128)} %copy-done.28) | copy-start | bytes 6148
  170.3 255.6 %reduce-scatter.24.cloned.1.call-start = ((), (), s32[]{:S(2)}) async-start(), calls=%async_computation.14 | async-start | bytes 442368 | tf_op jit(solution)/shard_map/reduce_scatter | solution.py:184
  187.1 37.9 %copy-start.27 = (f32[3072]{0:T(1024)S(1)}, f32[3072]{0:T(1024)}, u32[]{:S(2)}) copy-start(f32[3072]{0:T(1024)} %copy-done.26) | copy-start | bytes 36868
  187.1 37.9 %copy-start.30 = (f32[4,128]{1,0:T(4,128)S(1)}, f32[4,128]{1,0:T(4,128)}, u32[]{:S(2)}) copy-start(f32[4,128]{1,0:T(4,128)} %copy-done.28) | copy-start | bytes 6148
  224.9 366.7 %reduce-scatter.28.cloned.1.call-start = ((), (), s32[]{:S(2)}) async-start(), calls=%async_computation.16 | async-start | bytes 10616832 | tf_op jit(solution)/shard_map/reduce_scatter | solution.py:186
  225.0 11.1 %copy-start.19 = (f32[768]{0:T(1024)S(1)}, f32[768]{0:T(1024)}, u32[]{:S(2)}) copy-start(f32[768]{0:T(1024)} %copy-done.18) | copy-start | bytes 9220
  225.0 11.0 %copy-start.22 = (f32[4,128]{1,0:T(4,128)S(1)}, f32[4,128]{1,0:T(4,128)}, u32[]{:S(2)}) copy-start(f32[4,128]{1,0:T(4,128)} %copy-done.21) | copy-start | bytes 6148
  241.5 516.3 %reduce-scatter.32.cloned.1.call-start = ((), (), s32[]{:S(2)}) async-start(), calls=%async_computation.18 | async-start | bytes 10616832 | tf_op jit(solution)/shard_map/reduce_scatter | solution.py:187
  250.2 573.0 %reduce-scatter.34.cloned.1.call-start = ((), (), s32[]{:S(2)}) async-start(), calls=%async_computation.19 | async-start | bytes 491520
  292.2 532.6 %reduce-scatter.38.cloned.1.call-start = ((), (), s32[]{:S(2)}) async-start(), calls=%async_computation.21 | async-start | bytes 491520
  363.6 462.8 %reduce-scatter.36.cloned.1.call-start = ((), (), s32[]{:S(2)}) async-start(), calls=%async_computation.20 | async-start | bytes 81920
  427.4 427.6 %reduce-scatter.30.cloned.1.call-start = ((), (), s32[]{:S(2)}) async-start(), calls=%async_computation.17 | async-start | bytes 1474560 | tf_op jit(solution)/shard_map/reduce_scatter | solution.py:193
  591.7 292.1 %reduce-scatter.40.cloned.1.call-start = ((), (), s32[]{:S(2)}) async-start(), calls=%async_computation.22 | async-start | bytes 1474560
  760.6 7.1 copy-start.41
  760.6 7.7 copy-start.42
  760.6 9.6 %copy-start.31 = (f32[4,128]{1,0:T(4,128)S(1)}, f32[4,128]{1,0:T(4,128)}, u32[]{:S(2)}) copy-start(f32[4,128]{1,0:T(4,128)} %copy-done.28) | copy-start | bytes 6148
  770.2 4.0 copy-start.14
  770.2 4.0 copy-start.16
  770.2 4.6 copy-start.20
  770.2 5.0 copy-start.11
  770.2 5.0 copy-start.25
  823.2 61.2 %copy-start.37 = (f32[768]{0:T(1024)}, f32[768]{0:T(1024)S(1)}, u32[]{:S(2)}) copy-start(f32[768]{0:T(1024)S(1)} %get-tuple-element.536) | copy-start | bytes 9220
  (17 other events, 23.5 us)
Sparse Core Ops, SparseCore 0:
  15.1 42.2 all-gather.1
  151.4 67.2 reduce-scatter.19
  222.2 67.9 reduce-scatter.21
  293.6 68.0 reduce-scatter.25
  365.4 60.3 reduce-scatter.23
  429.3 162.3 reduce-scatter.27
  595.2 162.5 reduce-scatter.31
  760.3 19.8 reduce-scatter.33
  782.8 20.7 reduce-scatter.37
  806.5 19.4 reduce-scatter.35
  829.3 25.7 reduce-scatter.29
  858.0 25.7 reduce-scatter.39
where the time goes:
time: 897 us; the launch traced here: 892 us
  waiting for transfers between devices  614 us (68%)
  matrix products  115 us (13%)
  other arithmetic  59.7 us (7%)
  local copies, waits for them, and re-layouts  45.2 us (5%)
  blocking collectives  41.3 us (5%)
  between operations  15.3 us (2%)
    reduce_scatter x1, waiting for transfers between devices, body(): lax.psum_scatter(grad_w_up, 'seq', scatter_dimension=0, tiled=True)  164 us
    reduce_scatter x1, waiting for transfers between devices, body(): lax.psum_scatter(grad_w_down, 'seq', scatter_dimension=0, tiled=True)  160 us
    reduce_scatter x1, waiting for transfers between devices, body(): lax.psum_scatter(grad_w_out, 'seq', scatter_dimension=0, tiled=True)  69.5 us
    reduce_scatter x1, waiting for transfers between devices, body(): lax.psum_scatter(grad_w_keyval, 'seq', scatter_dimension=0, tiled=True)  62.1 us
    psum x1, blocking collectives, body(): lax.psum((grad_gain_one, grad_shift_one, grad_gain_two, grad_shift_two, g...  41.3 us
    reduce_scatter x1, waiting for transfers between devices, body(): lax.psum_scatter(grad_w_query, 'seq', scatter_dimension=0, tiled=True)  40 us
    reduce_scatter x1, waiting for transfers between devices, body(): d_kv = lax.psum_scatter(d_kv_terms, 'seq', scatter_dimension=1, tiled=True)  31.6 us
    unnamed x16, waiting for transfers between devices  28.9 us
  transfers between devices with their start and end apart: 12, of which 9 were waited for; matrix products, arithmetic and copies ran while one was open for 13% of the time, Pallas kernels for 0%

commit v1 on v0

--- a/solution.py
+++ b/solution.py
@@ -1,10 +1,431 @@
 import jax
 import jax.numpy as jnp
 from jax import lax
+from jax.experimental import pallas as pl
+from jax.experimental.pallas import tpu as pltpu
 from jax.sharding import PartitionSpec as P
 
 HEAD = 64
 ROT = 16
+MESH = pl.DeviceIdType.MESH
+BF = jnp.bfloat16
+F32 = jnp.float32
+
+
+def dot(a, b, ca=1, cb=0):
+    return lax.dot_general(a, b, (((ca,), (cb,)), ((), ())), preferred_element_type=F32)
+
+
+def gelu_pair(u):
+    cdf = 0.5 * (1.0 + lax.erf(u * 0.7071067811865476))
+    pdf = 0.3989422804014327 * jnp.exp(-0.5 * u * u)
+    return u * cdf, cdf + u * pdf
+
+
+def bit_of(value, bit):
+    return lax.rem(lax.div(value, 2**bit), 2)
+
+
+def flip(value, bit):
+    return value + (1 - 2 * bit_of(value, bit)) * 2**bit
+
+
+def put(value, bit, new):
+    return value + (new - bit_of(value, bit)) * 2**bit
+
+
+def placed(index, bits):
+    at = 0
+    for bit in bits:
+        at = at * 2 + (index >> bit) % 2
+    return at
+
+
+class Links:
+    def __init__(self, send, recv):
+        self.send, self.recv, self.used, self.waits = send, recv, 0, []
+
+    def take(self, count=1):
+        first = self.used
+        self.used += count
+        return first
+
+    def start(self, src, dst, device):
+        k = self.take()
+        copy = pltpu.make_async_remote_copy(
+            src_ref=src,
+            dst_ref=dst,
+            send_sem=self.send.at[k],
+            recv_sem=self.recv.at[k],
+            device_id=device,
+            device_id_type=MESH,
+        )
+        copy.start()
+        self.waits.append(copy)
+        return copy
+
+    def finish(self):
+        for copy in self.waits:
+            copy.wait_send()
+
+
+def halving(links, cur, stages, recvs):
+    blocks = cur.shape[0]
+    off = jnp.int32(0)
+    for (mine, partner), recv in zip(stages, recvs):
+        half = blocks // 2
+        copy = links.start(cur.at[pl.ds(off + (1 - mine) * half, half)], recv, partner)
+        yield None
+        copy.wait_recv()
+        off = off + mine * half
+
+        def add(i, _, off=off, recv=recv):
+            cur[off + i] = cur[off + i] + recv[i]
+            return 0
+
+        lax.fori_loop(0, half, add, 0)
+        blocks = half
+    yield off
+
+
+def kernel(sizes, x_hbm, g_hbm, lens, pars, wup_hbm, wdn_hbm, *rest):
+    NS, NJ, BS, BJ, SL, SPAN, D, FF = sizes
+    ROWS = SL * SPAN
+    HF = FF // 2
+    W = FF // NJ
+    MID = NJ // 4
+    R = D // NS
+    QN = NJ // 2
+    FRH = FF // NS // 2
+    DW = D // QN
+    (o_mlp, o_dmlp, o_up, o_dn, o_bup) = rest[:5]
+    (x, g, wup, wdn, mlp2, g2, act, dup, dmine, dsend, drecv, msend, mrecv) = rest[5:18]
+    ups, upr, dns, dnr = rest[18:20], rest[20:22], rest[22:24], rest[24:26]
+    (upm, dnp, dnm, sv, svr, send, recv, lsem) = rest[26:]
+    links = Links(send, recv)
+    s = lax.axis_index("seq")
+    j = lax.axis_index("slot")
+    c = bit_of(j, 0)
+    tj = bit_of(j, BJ - 1)
+    ts = bit_of(s, BS - 1)
+    buddy = (s, flip(j, 0))
+
+    loads = [
+        pltpu.make_async_copy(x_hbm, x, lsem.at[0]),
+        pltpu.make_async_copy(g_hbm, g, lsem.at[1]),
+        pltpu.make_async_copy(
+            wup_hbm.at[:, pl.ds(pl.multiple_of(c * HF, HF), HF)], wup, lsem.at[2]
+        ),
+        pltpu.make_async_copy(
+            wdn_hbm.at[pl.ds(pl.multiple_of(c * HF, HF), HF), :], wdn, lsem.at[3]
+        ),
+    ]
+    for copy in loads:
+        copy.start()
+
+    near = [(flip(s, b), j) for b in range(BS)] + [(s, flip(j, b)) for b in range(BJ)]
+    near += [(s, flip(flip(j, BJ - 1), 0)), (flip(s, BS - 1), flip(j, 0))]
+    barrier = pltpu.get_barrier_semaphore()
+    for device in near:
+        pl.semaphore_signal(barrier, inc=1, device_id=device, device_id_type=MESH)
+    pl.semaphore_wait(barrier, len(near))
+
+    sv[...] = jnp.zeros_like(sv)
+    loads[0].wait()
+    loads[1].wait()
+    spot = s * SPAN + lax.broadcasted_iota(jnp.int32, (SPAN, 1), 0)
+    for i in range(SL):
+        rows = pl.ds(i * SPAN, SPAN)
+        v = x[rows, :].astype(F32)
+        v = v - jnp.mean(v, axis=-1, keepdims=True)
+        v = v * lax.rsqrt(jnp.mean(v * v, axis=-1, keepdims=True) + 1e-05)
+        mlp2[rows, :] = (v * pars[2:3, :] + pars[3:4, :]).astype(BF)
+        g2[rows, :] = jnp.where(spot < lens[i], g[rows, :].astype(F32), 0.0).astype(BF)
+    own = pl.ds(0, ROWS)
+    theirs = pl.ds(ROWS, ROWS)
+    got_m = links.start(mlp2.at[own, :], mlp2.at[theirs, :], buddy)
+    got_g = links.start(g2.at[own, :], g2.at[theirs, :], buddy)
+    loads[2].wait()
+    loads[3].wait()
+
+    RB = 256
+    NB = 512
+
+    def first(i, _):
+        rows = pl.ds(pl.multiple_of(i * RB, RB), RB)
+        for f in range(HF // NB):
+            cols = slice(f * NB, (f + 1) * NB)
+            at = f * NB
+            bias = jnp.where(
+                c == 0,
+                pars[7 + at // D : 8 + at // D, at % D : at % D + NB]
+                if at % D + NB <= D
+                else jnp.concatenate(
+                    [
+                        pars[7 + at // D : 8 + at // D, at % D :],
+                        pars[8 + at // D : 9 + at // D, : NB - (D - at % D)],
+                    ],
+                    axis=1,
+                ),
+                pars[7 + (at + HF) // D : 8 + (at + HF) // D, (at + HF) % D : (at + HF) % D + NB]
+                if (at + HF) % D + NB <= D
+                else jnp.concatenate(
+                    [
+                        pars[7 + (at + HF) // D : 8 + (at + HF) // D, (at + HF) % D :],
+                        pars[
+                            8 + (at + HF) // D : 9 + (at + HF) // D,
+                            : NB - (D - (at + HF) % D),
+                        ],
+                    ],
+                    axis=1,
+                ),
+            )
+            up = dot(mlp2[rows, :], wup[:, cols]) + bias
+            back = dot(g2[rows, :], wdn[cols, :], 1, 1)
+            a, slope = gelu_pair(up)
+            act[rows, cols] = a.astype(BF)
+            dup[rows, cols] = (back * slope).astype(BF)
+        return 0
+
+    lax.fori_loop(0, ROWS // RB, first, 0)
+    got_m.wait_recv()
+    got_g.wait_recv()
+    lax.fori_loop(ROWS // RB, 2 * ROWS // RB, first, 0)
+
+    orders = [list(range(BS - 1)), list(range(BS - 1))]
+    if BS > 2:
+        orders[1] = orders[1][1:] + orders[1][:1]
+    for k in range(NS // 2):
+        ff = slice(k * 2 * FRH, (k + 1) * 2 * FRH)
+        part = dot(act[:, ff], g2[...], 0, 0).astype(BF)
+        for p in range(2):
+            at = placed(k, orders[p])
+            for q in range(QN):
+                dns[p][q * (NS // 2) + at] = part[p * FRH : (p + 1) * FRH, q * DW : (q + 1) * DW]
+    slot_bits = [(bit_of(j, b), (s, flip(j, b))) for b in range(BJ - 1, 0, -1)]
+    pipes = []
+    for p in range(2):
+        stages = slot_bits + [(bit_of(s, b), (flip(s, b), j)) for b in orders[p]]
+        recvs, at = [], 0
+        blocks = QN * NS // 2
+        for _ in stages:
+            blocks //= 2
+            recvs.append(dnr[p].at[pl.ds(at, blocks)])
+            at += blocks
+        pipes.append(halving(links, dns[p], stages, recvs))
+    for pipe in pipes:
+        next(pipe)
+    RK = 4 * R
+    for k in range(NS // 4):
+        for p in range(2):
+            for q in range(MID):
+                at = (q * 2 + p) * W
+                part = dot(mlp2[:, k * RK : (k + 1) * RK], dup[:, at : at + W], 0, 0).astype(BF)
+                for r in range(4):
+                    block = placed(k * 4 + r, orders[p] + [BS - 1]) * MID + q
+                    ups[p][block] = part[r * R : (r + 1) * R, :]
+    mid_bits = [(bit_of(j, b), (s, flip(j, b))) for b in range(BJ - 2, 0, -1)]
+    for p in range(2):
+        stages = [(bit_of(s, b), (flip(s, b), j)) for b in orders[p] + [BS - 1]] + mid_bits
+        recvs, at = [], 0
+        blocks = NS * MID
+        for _ in stages:
+            blocks //= 2
+            recvs.append(upr[p].at[pl.ds(at, blocks)])
+            at += blocks
+        pipes.append(halving(links, ups[p], stages, recvs))
+    for pipe in pipes[2:]:
+        next(pipe)
+
+    for k in range(ROWS // RB):
+        rows = slice(ROWS + k * RB, ROWS + (k + 1) * RB)
+        here = slice(k * RB, (k + 1) * RB)
+        msend[here, :] = dot(act[rows, :], wdn[...]).astype(BF)
+        dsend[here, :] = dot(dup[rows, :], wup[...], 1, 1).astype(BF)
+    got_out = links.start(msend, mrecv, buddy)
+    got_back = links.start(dsend, drecv, buddy)
+
+    half = jnp.sum(dup[...].astype(F32), axis=0, keepdims=True)
+    for q in range(FF // D):
+        piece = half[:, (q * D) % HF : (q * D) % HF + D]
+        sv[q : q + 1, :] = jnp.where(c == (q * D) // HF, piece, 0.0)
+
+    for k in range(ROWS // RB):
+        here = slice(k * RB, (k + 1) * RB)
+        o_mlp[here, :] = dot(act[here, :], wdn[...])
+        o_dmlp[here, :] = dot(dup[here, :], wup[...], 1, 1)
+    got_out.wait_recv()
+    got_back.wait_recv()
+    for k in range(ROWS // 128):
+        here = slice(k * 128, (k + 1) * 128)
+        o_mlp[here, :] = o_mlp[here, :] + mrecv[here, :].astype(F32)
+        o_dmlp[here, :] = o_dmlp[here, :] + drecv[here, :].astype(F32)
+
+    ends = [None] * 4
+    live = [0, 1, 2, 3]
+    while live:
+        for n in list(live):
+            ends[n] = next(pipes[n])
+            if ends[n] is not None:
+                live.remove(n)
+
+    def scatter_pair(src, dst, first_k, mine, target, is_self):
+        k = links.take()
+        remote = pltpu.make_async_remote_copy(
+            src_ref=src,
+            dst_ref=dst.at[mine],
+            send_sem=links.send.at[k],
+            recv_sem=links.recv.at[first_k + mine],
+            device_id=target,
+            device_id_type=MESH,
+        )
+        local = pltpu.make_async_copy(src, dst.at[mine], links.recv.at[first_k + mine])
+
+        @pl.when(is_self)
+        def _():
+            local.start()
+
+        @pl.when(jnp.logical_not(is_self))
+        def _():
+            remote.start()
+
+        def done():
+            @pl.when(jnp.logical_not(is_self))
+            def _():
+                remote.wait_send()
+
+        return done
+
+    dones, arrivals = [], []
+
+    def arrive(dst, first_k):
+        for t in range(2):
+            arrivals.append(
+                pltpu.make_async_copy(dst.at[t], dst.at[t], links.recv.at[first_k + t])
+            )
+
+    for p in range(2):
+        upp = upm[p]
+        upp[...] = ups[p][ends[2 + p]]
+    for p in range(2):
+        part = dns[p][ends[p]]
+        for h in range(2):
+            dnm[2 * p + h] = part[:, h * (DW // 2) : (h + 1) * (DW // 2)]
+    first_k = links.take(2)
+    for p in range(2):
+        is_self = jnp.logical_and(tj == c, c == p)
+        target = (s, put(put(j, 0, p), BJ - 1, c))
+        dones.append(scatter_pair(upm[p], upm[2], first_k, tj, target, is_self))
+    arrive(upm[2], first_k)
+    for p in range(2):
+        first_k = links.take(2)
+        for h in range(2):
+            is_self = jnp.logical_and(ts == c, c == h)
+            target = (put(s, BS - 1, c), put(j, 0, h))
+            dones.append(
+                scatter_pair(dnm.at[2 * p + h], dnp.at[p], first_k, ts, target, is_self)
+            )
+        arrive(dnp.at[p], first_k)
+
+    stages = [(s, flip(j, b)) for b in range(BJ)] + [(flip(s, b), j) for b in range(BS)]
+    for n, partner in enumerate(stages):
+        out = svr.at[2 * n]
+        out[...] = sv[...]
+        copy = links.start(out, svr.at[2 * n + 1], partner)
+        copy.wait_recv()
+        sv[...] = sv[...] + svr[2 * n + 1]
+    o_bup[...] = sv[...]
+    for copy in arrivals:
+        copy.wait()
+    o_up[...] = upm[2][0].astype(F32) + upm[2][1].astype(F32)
+    for p in range(2):
+        o_dn[p * FRH : (p + 1) * FRH, :] = dnp[p, 0].astype(F32) + dnp[p, 1].astype(F32)
+    for done in dones:
+        done()
+    links.finish()
+
+
+def mlp_call(mesh_sizes, x, g, lengths, pars, w_up, w_down):
+    NS, NJ = mesh_sizes
+    BS, BJ = NS.bit_length() - 1, NJ.bit_length() - 1
+    SL, SPAN, D = x.shape
+    FF = w_up.shape[1]
+    ROWS = SL * SPAN
+    HF, W, MID, R, QN, FRH, DW = (
+        FF // 2,
+        FF // NJ,
+        NJ // 4,
+        D // NS,
+        NJ // 2,
+        FF // NS // 2,
+        2 * D // NJ,
+    )
+    vm = pltpu.VMEM
+    n_stage = BS + BJ
+    scratch = [
+        vm((ROWS, D), BF),
+        vm((ROWS, D), BF),
+        vm((D, HF), BF),
+        vm((HF, D), BF),
+        vm((2 * ROWS, D), BF),
+        vm((2 * ROWS, D), BF),
+        vm((2 * ROWS, HF), BF),
+        vm((2 * ROWS, HF), BF),
+        vm((8, 128), F32),
+        vm((ROWS, D), BF),
+        vm((ROWS, D), BF),
+        vm((ROWS, D), BF),
+        vm((ROWS, D), BF),
+        vm((NS * MID, R, W), BF),
+        vm((NS * MID, R, W), BF),
+        vm((NS * MID, R, W), BF),
+        vm((NS * MID, R, W), BF),
+        vm((QN * NS // 2, FRH, DW), BF),
+        vm((QN * NS // 2, FRH, DW), BF),
+        vm((QN * NS // 2, FRH, DW), BF),
+        vm((QN * NS // 2, FRH, DW), BF),
+        vm((4, R, W), BF),
+        vm((2, 2, FRH, DW // 2), BF),
+        vm((4, FRH, DW // 2), BF),
+        vm((8, D), F32),
+        vm((2 * n_stage, 8, D), F32),
+        pltpu.SemaphoreType.DMA((64,)),
+        pltpu.SemaphoreType.DMA((64,)),
+        pltpu.SemaphoreType.DMA((4,)),
+    ]
+    sizes = (NS, NJ, BS, BJ, SL, SPAN, D, FF)
+
+    def call(*refs):
+        refs = list(refs)
+        at = 11 + 21
+        upm = refs[at]
+        refs[at] = [upm.at[0], upm.at[1], upm.at[pl.ds(2, 2)]]
+        kernel(sizes, *refs)
+
+    anyspace = pl.BlockSpec(memory_space=pl.ANY)
+    return pl.pallas_call(
+        call,
+        out_shape=[
+            jax.ShapeDtypeStruct((ROWS, D), F32),
+            jax.ShapeDtypeStruct((ROWS, D), F32),
+            jax.ShapeDtypeStruct((R, W), F32),
+            jax.ShapeDtypeStruct((2 * FRH, DW // 2), F32),
+            jax.ShapeDtypeStruct((8, D), F32),
+        ],
+        in_specs=[
+            anyspace,
+            anyspace,
+            pl.BlockSpec(memory_space=pltpu.SMEM),
+            pl.BlockSpec(memory_space=pltpu.VMEM),
+            anyspace,
+            anyspace,
+        ],
+        out_specs=[pl.BlockSpec(memory_space=pltpu.VMEM)] * 5,
+        scratch_shapes=scratch,
+        compiler_params=pltpu.CompilerParams(
+            collective_id=0, has_side_effects=True, vmem_limit_bytes=60 * 2**20
+        ),
+    )(x.reshape(ROWS, D), g.reshape(ROWS, D), lengths, pars, w_up, w_down)
 
 
 def norm(value, gain, bias):
@@ -26,10 +447,6 @@
     part = value[..., :ROT]
     swapped = jnp.concatenate([-part[..., half:], part[..., :half]], axis=-1)
     return jnp.concatenate([part * cosine + swapped * sine, value[..., ROT:]], axis=-1)
-
-
-def exact_gelu(value):
-    return jax.nn.gelu(value, approximate=False)
 
 
 def body(
@@ -80,10 +497,22 @@
     key_turned, key_back = jax.vjp(lambda v: turn(v, cosine, sine), kv_pre[..., :HEAD])
     kv_local = jnp.concatenate([key_turned, kv_pre[..., HEAD:]], axis=-1).astype(jnp.bfloat16)
     kv_whole = lax.all_gather(kv_local, "seq", axis=1, tiled=True)
-    up_pre = jnp.dot(mlp_in, w_up, preferred_element_type=jnp.float32) + b_up.astype(jnp.float32)
-    act32, gelu_back = jax.vjp(exact_gelu, up_pre)
-    act = act32.astype(jnp.bfloat16)
-    mlp_out = jnp.dot(act, w_down, preferred_element_type=jnp.float32) + b_down.astype(jnp.float32)
+    pars = jnp.concatenate(
+        [
+            v.astype(jnp.float32)
+            for v in (ln1_gain, ln1_bias, ln2_gain, ln2_bias, b_query, b_out, b_down, b_up)
+        ]
+    ).reshape(7 + b_up.shape[0] // width, width)
+    mlp_part, d_mlp, up_part, down_part, bup = mlp_call(
+        (lax.axis_size("seq"), lax.axis_size("slot")),
+        hidden_in,
+        out_grad,
+        lengths,
+        pars,
+        w_up,
+        w_down,
+    )
+    mlp_out = mlp_part.reshape(hidden.shape) + b_down.astype(jnp.float32)
 
     def scores_of(query_slot, kv_slot, length):
         raw = (
@@ -115,12 +544,8 @@
     grad_bias_out = jnp.sum(grad_full, axis=(0, 1))
     grad_w_out = jnp.einsum("std,ste->de", attn, grad_low, preferred_element_type=jnp.float32)
     d_attn = jnp.dot(grad_low, w_out.T, preferred_element_type=jnp.float32).astype(jnp.bfloat16)
-    grad_w_down = jnp.einsum("stf,ste->fe", act, grad_low, preferred_element_type=jnp.float32)
-    d_act = jnp.dot(grad_low, w_down.T, preferred_element_type=jnp.float32)
-    d_up = gelu_back(d_act)[0].astype(jnp.bfloat16)
-    grad_b_up = jnp.sum(d_up.astype(jnp.float32), axis=(0, 1))
-    grad_w_up = jnp.einsum("std,stf->df", mlp_in, d_up, preferred_element_type=jnp.float32)
-    d_mlp_in = jnp.dot(d_up, w_up.T, preferred_element_type=jnp.float32)
+    d_mlp_in = d_mlp.reshape(hidden.shape)
+    grad_b_up = bup[: b_up.shape[0] // width].reshape(b_up.shape)
 
     def backward_slot(item):
         query_slot, kv_slot, length, log_total, d_slot = item
@@ -174,24 +599,18 @@
             grad_b_query,
             grad_b_keyval,
             grad_bias_out,
-            grad_b_up,
-            grad_bias_out,
         ),
         ("seq", "slot"),
     )
-    query_rows, keyval_rows, out_rows, up_rows, down_rows = (
+    query_rows, keyval_rows, out_rows = (
         lax.psum_scatter(grad_w_query, "seq", scatter_dimension=0, tiled=True),
         lax.psum_scatter(grad_w_keyval, "seq", scatter_dimension=0, tiled=True),
         lax.psum_scatter(grad_w_out, "seq", scatter_dimension=0, tiled=True),
-        lax.psum_scatter(grad_w_up, "seq", scatter_dimension=0, tiled=True),
-        lax.psum_scatter(grad_w_down, "seq", scatter_dimension=0, tiled=True),
-    )
-    query_part, keyval_part, out_part, up_part, down_part = (
+    )
+    query_part, keyval_part, out_part = (
         lax.psum_scatter(query_rows, "slot", scatter_dimension=1, tiled=True),
         lax.psum_scatter(keyval_rows, "slot", scatter_dimension=1, tiled=True),
         lax.psum_scatter(out_rows, "slot", scatter_dimension=1, tiled=True),
-        lax.psum_scatter(up_rows, "slot", scatter_dimension=1, tiled=True),
-        lax.psum_scatter(down_rows, "slot", scatter_dimension=1, tiled=True),
     )
     return (
         layer_out,
@@ -207,9 +626,9 @@
         out_part,
         small[6],
         up_part,
-        small[7],
+        grad_b_up,
         down_part,
-        small[8],
+        small[6],
     )
 
 

time: 897 us -> 526 us (0.59)
  waiting for transfers between devices: 614 us -> 195 us
  Pallas kernels: 0 us -> 104 us
  matrix products: 115 us -> 71.4 us
  other arithmetic: 59.7 us -> 43 us
    reduce_scatter x3 -> x0, waiting for transfers between devices: 353 us -> none  [the longest x1 164 us: body(): lax.psum_scatter(grad_w_up, 'seq', scatter_dimension=0, tiled=True)]
    pallas_call x0 -> x1, Pallas kernels: none -> 104 us  [mlp_call(): pl.pallas_call(call, out_shape=[jax.ShapeDtypeStruct((ROWS, D), F32), jax...]
    dot_general x6 -> x0, matrix products: 45.5 us -> none  [the longest x1 9.37 us: body(): d_act = jnp.dot(grad_low, w_down.T, preferred_element_type=jnp.float32)]
    reduce_scatter x1, waiting for transfers between devices: 40 us -> 0.01 us  [body(): lax.psum_scatter(grad_w_query, 'seq', scatter_dimension=0, tiled=True)]
    reduce_scatter x1, waiting for transfers between devices: 69.5 us -> 33.6 us  [body(): lax.psum_scatter(grad_w_out, 'seq', scatter_dimension=0, tiled=True)]
    reduce_scatter x1, waiting for transfers between devices: 31.6 us -> 55.4 us  [body(): d_kv = lax.psum_scatter(d_kv_terms, 'seq', scatter_dimension=1, tiled=True)]
    convert_element_type x5 -> x2, other arithmetic: 17.4 us -> 0.6 us  [body(): v.astype(jnp.float32)]
    unnamed x16 -> x11, waiting for transfers between devices: 28.9 us -> 18.3 us
  transfers between devices with their start and end apart: 12 -> 8, of which waited for: 9 -> 5; matrix products, arithmetic and copies ran while one was open for 13% -> 11% of each run, Pallas kernels for 0% -> 20%
where the time goes in v1:
time: 526 us; the launch traced here: 521 us
  waiting for transfers between devices  195 us (37%)
  Pallas kernels  104 us (20%)
  matrix products  71.4 us (14%)
  local copies, waits for them, and re-layouts  50.1 us (10%)
  other arithmetic  43 us (8%)
  blocking collectives  41.2 us (8%)
  between operations  15.4 us (3%)
    pallas_call x1, Pallas kernels, mlp_call(): pl.pallas_call(call, out_shape=[jax.ShapeDtypeStruct((ROWS, D), F32), jax...  104 us
    reduce_scatter x1, waiting for transfers between devices, body(): lax.psum_scatter(grad_w_keyval, 'seq', scatter_dimension=0, tiled=True)  57.8 us
    reduce_scatter x1, waiting for transfers between devices, body(): d_kv = lax.psum_scatter(d_kv_terms, 'seq', scatter_dimension=1, tiled=True)  55.4 us
    psum x1, blocking collectives, body(): lax.psum((grad_gain_one, grad_shift_one, grad_gain_two, grad_shift_two, g...  41.2 us
    reduce_scatter x1, waiting for transfers between devices, body(): lax.psum_scatter(grad_w_out, 'seq', scatter_dimension=0, tiled=True)  33.6 us
    all_gather x1, waiting for transfers between devices, body(): kv_whole = lax.all_gather(kv_local, 'seq', axis=1, tiled=True)  29.5 us
    unnamed x114, local copies, waits for them, and re-layouts  19 us
    unnamed x11, waiting for transfers between devices  18.3 us
  transfers between devices with their start and end apart: 8, of which 5 were waited for; matrix products, arithmetic and copies ran while one was open for 11% of the time, Pallas kernels for 20%

profile of v1, /device:TPU:0, one launch (start us, length us, event | category | flops | bytes accessed | tf_op | source)
XLA Modules:
  0.0 520.8 jit_solution(6441556027386504989)
XLA Ops:
  12.5 2.1 convolution_add_fusion.1
  14.6 2.0 copy.73
  18.8 3.0 convolution_convert_fusion
  21.8 2.3 copy.75
  25.3 29.5 %all-gather.2.cloned.1.call-done = bf16[4,1024,128]{1,2,0:T(8,128)(2,1)} async-done(((bf16[4,128,128]{1,2,0:T(8,128)(2,1)}), bf16[4,1024,128]{1,2,0:T(8,128)(2,1)}) %all-gather.2.cloned.1.call-update) | async-done | bytes 1048592 | tf_op jit(solution)/shard_map/all_gather | solution.py:499
  54.8 33.7 %while.28 = (s32[]{:T(128)}, bf16[4,128,768]{1,2,0:T(8,128)(2,1)}, f32[4,12,128,1]{2,1,3,0:T(8,128)}, bf16[4,1024,128]{1,2,0:T(8,128)(2,1)}, s32[4]{0:T(128)}, /...) while((s32[]{:T(128)}, bf16[4,128,768]{1,2,0:T(8,128)(2,1)}, ...), condition=%wide.region_5.6_spmd.clone.clone, body=%wide.region_2.5_spmd.clone.clone.sunk | while | flops 421887616 | bytes 21031024 | solution.py:539
  60.9 1.7 fusion.125
  69.3 1.7 fusion.125
  77.7 1.7 fusion.125
  86.1 1.7 fusion.125
  88.5 61.7 %while.29 = (s32[]{:T(128)}, f32[4,128,12,64]{1,3,2,0:T(8,128)}, f32[4,1024,128]{1,2,0:T(8,128)}, bf16[4,1024,128]{1,2,0:T(8,128)(2,1)}, s32[4]{0:T(128)}, /*ind...) while((s32[]{:T(128)}, f32[4,128,12,64]{1,3,2,0:T(8,128)}, ...), condition=%wide.region_8.9_spmd.clone.clone, body=%wide.region_6.8_spmd.clone.clone.sunk | while | flops 1030782592 | bytes 57722648 | solution.py:576
  92.9 2.7 fusion.134
  95.5 1.7 fusion.135
  97.2 2.0 fusion.138
  99.2 2.5 fusion.137
  108.3 2.7 fusion.134
  111.0 1.7 fusion.135
  112.6 2.0 fusion.138
  114.6 2.5 fusion.137
  123.7 2.7 fusion.134
  126.4 1.7 fusion.135
  128.1 2.0 fusion.138
  130.1 2.5 fusion.137
  139.1 2.7 fusion.134
  141.8 1.7 fusion.135
  143.5 2.0 fusion.138
  145.5 2.5 fusion.137
  153.8 2.5 convolution_bitcast_fusion.2
  157.7 3.0 convolution_bitcast_fusion.1
  162.1 55.4 %reduce-scatter.14.cloned.1.call-done = f32[4,128,128]{1,2,0:T(8,128)} async-done(((f32[4,1024,128]{1,2,0:T(8,128)}), f32[4,128,128]{1,2,0:T(8,128)}) %reduce-scatter.14.cloned.1.call-update) | async-done | bytes 262160 | tf_op jit(solution)/shard_map/reduce_scatter | solution.py:579
  223.2 103.9 %shard_map.288 = (f32[512,768]{1,0:T(8,128)}, f32[512,768]{1,0:T(8,128)}, f32[96,768]{1,0:T(8,128)}, f32[384,192]{1,0:T(8,128)}, f32[8,768]{1,0:T(8,128)}) custom-call(bf16[512,768]{1,0:T(8,128)(2,1)} %bitcast.207, bf16[512,768]{1,0:T(8,128)(2,1)} %bitcast.208, s32[4]{0:T(128)S(1)} %copy-done.53, f32[11,768]{1,0:T(8,128)} %reshape.392.refs_3_, ...), custom_call_target="tpu_custom_call" | custom-call | tf_op jit(solution)/shard_map/pallas_call | solution.py:406
  327.1 1.9 copy.83
  330.4 2.2 reduce_sum.151
  333.3 3.6 fusion.71
  337.0 1.5 fusion.80
  338.5 1.9 copy.97
  340.5 4.6 fusion.95
  345.7 33.6 %reduce-scatter.20.cloned.1.call-done = f32[96,768]{1,0:T(8,128)} async-done(((f32[768,768]{1,0:T(8,128)}), f32[96,768]{1,0:T(8,128)}) %reduce-scatter.20.cloned.1.call-update) | async-done | bytes 294928 | tf_op jit(solution)/shard_map/reduce_scatter | solution.py:608
  379.4 1.9 copy.101
  381.3 3.1 fusion.64
  385.1 57.8 %reduce-scatter.18.cloned.1.call-done = f32[96,128]{1,0:T(8,128)} async-done(((f32[768,128]{1,0:T(8,128)}), f32[96,128]{1,0:T(8,128)}) %reduce-scatter.18.cloned.1.call-update) | async-done | bytes 49168 | tf_op jit(solution)/shard_map/reduce_scatter | solution.py:607
  442.9 1.5 copy.99
  444.5 4.0 convert_reduce_fusion.1
  448.6 41.2 %all-reduce.8 = (f32[768]{0:T(1024)}, f32[768]{0:T(1024)}, f32[768]{0:T(1024)}, f32[768]{0:T(1024)}, f32[768]{0:T(1024)}, /*index=5*/f32[128]{0:T(128)}, f32[768]{0:T(1024)S(1)}) all-reduce(f32[768]{0:T(1024)} %get-tuple-element.273, f32[768]{0:T(1024)} %get-tuple-element.275, ...), channel_id=1, replica_groups=mesh['seq'=8,'slot'=4] {'seq','slot'}, use_global_device_ids=true, to_apply=%region_15.16 | all-reduce | flops 4736 | bytes 37888 | tf_op jit(solution)/shard_map/psum | solution.py:593
  489.8 1.6 copy.98
  491.4 1.6 copy.102
  493.1 18.2 %reduce-scatter.24.cloned.1.call-done = f32[32,96]{1,0:T(8,128)} async-done(((f32[128,96]{1,0:T(8,128)}), f32[32,96]{1,0:T(8,128)}) %reduce-scatter.24.cloned.1.call-update) | async-done | bytes 12304
  511.8 1.7 copy.138
  (280 shorter events, 77.0 us)
Async XLA Ops:
  7.2 5.3 %copy-start = (bf16[768,768]{1,0:T(8,128)(2,1)S(1)}, bf16[768,768]{1,0:T(8,128)(2,1)}, u32[]{:S(2)}) copy-start(bf16[768,768]{1,0:T(8,128)(2,1)} %param.28) | copy-start | bytes 3538948
  7.2 3.7 copy-start.2
  7.2 3.1 copy-start.38
  7.2 3.1 copy-start.40
  7.2 3.6 copy-start.55
  7.2 3.6 copy-start.19
  7.3 47.5 %all-gather.2.cloned.1.call-start = ((), (), s32[]{:S(2)}) async-start(), calls=%async_computation.7 | async-start | bytes 1179648 | tf_op jit(solution)/shard_map/all_gather | solution.py:499
  8.8 3.7 copy-start.26
  10.3 2.2 copy-start.33
  10.3 2.2 copy-start.21
  12.4 205.2 %reduce-scatter.14.cloned.1.call-start = ((), (), s32[]{:S(2)}) async-start(), calls=%async_computation.8 | async-start | bytes 2359296 | tf_op jit(solution)/shard_map/reduce_scatter | solution.py:579
  14.6 4.2 copy-start.7
  88.5 2.2 copy-start.5
  103.9 2.2 copy-start.5
  119.4 2.2 copy-start.5
  134.8 2.2 copy-start.5
  150.2 188.3 %reduce-scatter.16.cloned.1.call-start = ((), (), s32[]{:S(2)}) async-start(), calls=%async_computation.9 | async-start | bytes 2654208 | tf_op jit(solution)/shard_map/reduce_scatter | solution.py:606
  151.8 1.9 copy-start.3
  151.8 1.9 copy-start.22
  151.8 1.9 copy-start.27
  151.8 1.9 copy-start.34
  151.9 1.9 copy-start.49
  156.3 223.0 %reduce-scatter.20.cloned.1.call-start = ((), (), s32[]{:S(2)}) async-start(), calls=%async_computation.11 | async-start | bytes 2654208 | tf_op jit(solution)/shard_map/reduce_scatter | solution.py:608
  160.7 60.2 %copy-start.23 = (f32[768]{0:T(1024)S(1)}, f32[768]{0:T(1024)}, u32[]{:S(2)}) copy-start(f32[768]{0:T(1024)} %copy-done.21) | copy-start | bytes 9220
  160.7 60.2 %copy-start.28 = (f32[4,128]{1,0:T(4,128)S(1)}, f32[4,128]{1,0:T(4,128)}, u32[]{:S(2)}) copy-start(f32[4,128]{1,0:T(4,128)} %copy-done.26) | copy-start | bytes 6148
  160.8 60.2 %copy-start.35 = (f32[4,128]{1,0:T(4,128)S(1)}, f32[4,128]{1,0:T(4,128)}, u32[]{:S(2)}) copy-start(f32[4,128]{1,0:T(4,128)} %copy-done.33) | copy-start | bytes 6148
  160.8 60.2 %copy-start.50 = (f32[768]{0:T(1024)S(1)}, f32[768]{0:T(1024)}, u32[]{:S(2)}) copy-start(f32[768]{0:T(1024)} %copy-done.48) | copy-start | bytes 9220
  160.8 282.1 %reduce-scatter.18.cloned.1.call-start = ((), (), s32[]{:S(2)}) async-start(), calls=%async_computation.10 | async-start | bytes 442368 | tf_op jit(solution)/shard_map/reduce_scatter | solution.py:607
  219.4 3.1 copy-start.16
  221.0 106.1 %copy-start.13 = (bf16[4,128,64]{1,2,0:T(8,128)(2,1)}, bf16[4,128,64]{1,2,0:T(8,128)(2,1)S(1)}, u32[]{:S(2)}) copy-start(bf16[4,128,64]{1,2,0:T(8,128)(2,1)S(1)} %add_convert_fusion.1) | copy-start | bytes 196612
  221.0 2.2 copy-start.53
  222.5 267.3 %reduce-scatter.22.cloned.1.call-start = ((), (), s32[]{:S(2)}) async-start(), calls=%async_computation.12 | async-start | bytes 491520
  327.1 5.5 %copy-start.32 = (f32[12,64]{1,0:T(8,128)S(1)}, f32[12,64]{1,0:T(8,128)}, u32[]{:S(2)}) copy-start(f32[12,64]{1,0:T(8,128)} %get-tuple-element.319) | copy-start | bytes 9220
  327.1 6.2 %copy-start.4 = (bf16[4,128,768]{2,1,0:T(8,128)(2,1)S(1)}, bf16[4,128,768]{2,1,0:T(8,128)(2,1)}, u32[]{:S(2)}) copy-start(bf16[4,128,768]{2,1,0:T(8,128)(2,1)} %param.21) | copy-start | bytes 2359300
  327.1 6.1 %copy-start.31 = (f32[4,128]{1,0:T(4,128)S(1)}, f32[4,128]{1,0:T(4,128)}, u32[]{:S(2)}) copy-start(f32[4,128]{1,0:T(4,128)} %copy-done.30) | copy-start | bytes 6148
  333.3 3.7 copy-start.14
  333.3 3.7 copy-start.17
  333.3 3.6 copy-start.20
  336.9 3.6 copy-start.1
  336.9 3.6 copy-start.24
  336.9 3.6 copy-start.25
  337.0 3.6 copy-start.29
  340.4 151.0 %reduce-scatter.26.cloned.1.call-start = ((), (), s32[]{:S(2)}) async-start(), calls=%async_computation.14 | async-start | bytes 491520
  340.5 4.6 copy-start.37
  381.3 129.9 %reduce-scatter.24.cloned.1.call-start = ((), (), s32[]{:S(2)}) async-start(), calls=%async_computation.13 | async-start | bytes 81920
  444.5 4.0 copy-start.15
  444.5 4.0 copy-start.18
  489.8 23.7 %copy-start.51 = (f32[768]{0:T(1024)}, f32[768]{0:T(1024)S(1)}, u32[]{:S(2)}) copy-start(f32[768]{0:T(1024)S(1)} %get-tuple-element.561) | copy-start | bytes 9220
  (25 other events, 30.2 us)
Sparse Core Ops, SparseCore 0:
  12.5 42.2 all-gather.1
  150.4 67.1 reduce-scatter.13
  221.1 84.8 reduce-scatter.15
  309.2 70.0 reduce-scatter.19
  382.5 60.3 reduce-scatter.17
  445.3 19.8 reduce-scatter.21
  467.7 21.1 reduce-scatter.25
  491.8 19.3 reduce-scatter.23

commit v2 on v0

v2 whole, which is shorter than its diff:
```python
import math

import jax
import jax.numpy as jnp
import numpy as np
from jax import lax
from jax.experimental import pallas as pl
from jax.experimental.pallas import tpu as pltpu
from jax.sharding import PartitionSpec as P

HEAD = 64
ROT = 16
PAIR = 2 * HEAD
MESH = pl.DeviceIdType.MESH
BF = jnp.bfloat16
F32 = jnp.float32


def dot(a, b, ca=1, cb=0):
    return lax.dot_general(a, b, (((ca,), (cb,)), ((), ())), preferred_element_type=F32)


def gelu_pair(u):
    cdf = 0.5 * (1.0 + lax.erf(u * 0.7071067811865476))
    pdf = 0.3989422804014327 * jnp.exp(-0.5 * u * u)
    return u * cdf, cdf + u * pdf


def bit_of(value, bit):
    return lax.rem(lax.div(value, 2**bit), 2)


def flip(value, bit):
    return value + (1 - 2 * bit_of(value, bit)) * 2**bit


def put(value, bit, new):
    return value + (new - bit_of(value, bit)) * 2**bit


def placed(index, bits):
    at = 0
    for bit in bits:
        at = at * 2 + (index >> bit) % 2
    return at


def turned(value, tables):
    same, after, before = tables
    return value * same + pltpu.roll(value, PAIR - 8, 1) * after + pltpu.roll(value, 8, 1) * before


def turned_back(value, tables):
    same, after, before = tables
    return (
        value * same
        + pltpu.roll(value * after, 8, 1)
        + pltpu.roll(value * before, PAIR - 8, 1)
    )


def rotary_tables(length):
    half = ROT // 2
    inverse = (10000.0 ** (-(np.arange(half, dtype=np.float32) * 2.0 / ROT))).astype(np.float32)
    turns = np.arange(length, dtype=np.float32)[:, None] * inverse[None, :]
    cosine = np.cos(turns.astype(np.float64)).astype(np.float32)
    sine = np.sin(turns.astype(np.float64)).astype(np.float32)
    out = np.zeros((3, length, PAIR), np.float32)
    out[0] = 1.0
    for head in range(2):
        at = head * HEAD
        out[0, :, at : at + half] = cosine
        out[0, :, at + half : at + ROT] = cosine
        out[1, :, at : at + half] = -sine
        out[2, :, at + half : at + ROT] = sine
    return out


class Links:
    def __init__(self, send, recv):
        self.send, self.recv, self.used, self.waits = send, recv, 0, []

    def take(self, count=1):
        first = self.used
        self.used += count
        return first

    def copy(self, src, dst, device, arrival=None):
        k = self.take()
        return pltpu.make_async_remote_copy(
            src_ref=src,
            dst_ref=dst,
            send_sem=self.send.at[k],
            recv_sem=self.recv.at[k if arrival is None else arrival],
            device_id=device,
            device_id_type=MESH,
        )

    def start(self, src, dst, device):
        copy = self.copy(src, dst, device)
        copy.start()
        self.waits.append(copy)
        return copy

    def unless(self, own, src, dst, device, arrival):
        remote = self.copy(src, dst, device, arrival)
        local = pltpu.make_async_copy(src, dst, self.recv.at[arrival])
        other = jnp.logical_not(own)
        self.waits.append((other, remote))

        def start():
            @pl.when(own)
            def _():
                local.start()

            @pl.when(other)
            def _():
                remote.start()

        return start

    def arrived(self, dst, arrival):
        pltpu.make_async_copy(dst, dst, self.recv.at[arrival]).wait()

    def finish(self):
        for copy in self.waits:
            if isinstance(copy, tuple):

                @pl.when(copy[0])
                def _(copy=copy):
                    copy[1].wait_send()

            else:
                copy.wait_send()


class Halving:
    def __init__(self, links, cur, stages, recv):
        blocks = cur.shape[0]
        off, at = jnp.int32(0), 0
        self.cur, self.steps, self.links = cur, [], links
        for mine, partner in stages:
            blocks //= 2
            src = cur.at[pl.ds(off + (1 - mine) * blocks, blocks)]
            dst = recv.at[pl.ds(at, blocks)]
            off = off + mine * blocks
            self.steps.append((links.copy(src, dst, partner), dst, off, blocks))
            at += blocks
        self.end = off

    def start(self, k):
        self.steps[k][0].start()
        self.links.waits.append(self.steps[k][0])

    def finish(self, k):
        copy, recv, off, blocks = self.steps[k]
        cur = self.cur
        copy.wait_recv()

        def add(i, _):
            cur[off + i] = cur[off + i] + recv[i]
            return 0

        lax.fori_loop(0, blocks, add, 0)

    def step(self, k):
        if k:
            self.finish(k - 1)
        if k < len(self.steps):
            self.start(k)


class Direct:
    def __init__(self, links, size, me, device_of, source, dst):
        self.links, self.size, self.me, self.dst = links, size, me, dst
        self.source = source
        self.out = []
        for d in range(1, size):
            target = lax.rem(me + d, size)
            self.out.append(links.copy(source(target), dst.at[me], device_of(target)))

    def start(self):
        for copy in self.out:
            copy.start()
            self.links.waits.append(copy)

    def finish(self):
        for d in range(1, self.size):
            sender = lax.rem(self.me + self.size - d, self.size)
            self.out[d - 1].wait_recv()


class Sizes:
    def __init__(self, NS, NJ, SL, SPAN, D, FF):
        self.NS, self.NJ, self.SL, self.SPAN, self.D, self.FF = NS, NJ, SL, SPAN, D, FF
        self.BS, self.BJ = NS.bit_length() - 1, NJ.bit_length() - 1
        self.ROWS, self.LEN, self.HF = SL * SPAN, NS * SPAN, FF // 2
        self.QN = NJ // 2
        self.R, self.W = D // NS, FF // NJ
        self.CH = NS // 2
        self.CW = self.HF // self.CH
        self.CPP = self.W // self.CW
        self.FRH, self.DW = self.CW // 2, D // self.QN
        self.R2, self.C4 = self.R // 2, D // NJ
        self.PAIRS = D // PAIR
        self.PG = self.PAIRS // 2
        self.PR = self.PG * SPAN
        self.KR = PAIR // NJ
        self.STEP = self.PG if self.LEN <= 1024 else 1


def scratch_of(z):
    vm = pltpu.VMEM
    rows, d = z.ROWS, z.D
    return dict(
        x=vm((rows, d), BF),
        g2=vm((2 * rows, d), BF),
        mlp2=vm((2 * rows, d), BF),
        ain=vm((rows, d), BF),
        wq=vm((d, d), BF),
        wkv=vm((d, PAIR), BF),
        wout=vm((d, d), BF),
        wup=vm((d, z.HF), BF),
        wdn=vm((z.HF, d), BF),
        tab=vm((3, z.SPAN, PAIR), F32),
        act=vm((2 * rows, z.HF), BF),
        dup=vm((2 * rows, z.HF), BF),
        l1=vm((2, z.SL, 2 * z.PR, PAIR), BF),
        l2=vm((2, z.SL, 2 * z.PR, PAIR), BF),
        att=vm((rows, d), BF),
        dq=vm((rows, d), BF),
        kv=vm((z.SL, z.NS, z.SPAN, PAIR), BF),
        kvs=vm((z.LEN, PAIR), BF),
        vks=vm((z.LEN, PAIR), BF),
        r1=vm((2 * z.STEP * z.SPAN, z.LEN), BF),
        r2=vm((2 * z.STEP * z.SPAN, z.LEN), BF),
        bias=vm((z.SPAN, z.LEN), F32),
        dkt=vm((z.SL, PAIR, z.LEN), F32 if z.LEN <= 1024 else BF),
        dks=vm((z.SL, z.NS, PAIR, z.SPAN), BF),
        dkr=vm((z.SL, z.NS - 1, PAIR, z.SPAN), BF),
        up=vm((z.CH, z.NS, z.R, z.CW), BF),
        upr=vm((z.CH, z.NS - 1, z.R, z.CW), BF),
        upf=vm((z.CPP, z.QN, z.R, z.CW), BF),
        dn=vm((z.CH, 2, z.QN, z.FRH, z.DW), BF),
        dnr=vm((z.CH, 2, z.QN - 1, z.FRH, z.DW), BF),
        dnr2=vm((2 * z.CH - 2, z.FRH, z.DW), BF),
        dnm=vm((4, z.FRH, z.DW // 2), BF),
        dnf=vm((2, 2, z.FRH, z.DW // 2), BF),
        wo=vm((2, z.NS, z.R2, d), BF),
        wor=vm((2, z.NS - 1, z.R2, d), BF),
        wos=vm((2, z.NJ, z.R2, z.C4), BF),
        wof=vm((2, z.NJ, z.R2, z.C4), BF),
        wox=vm((2, 2, z.R2, z.C4), F32),
        woy=vm((2, 2, z.R2, z.C4), BF),
        gq=vm((2, 2 * z.NS, z.R2, d // 2), BF),
        gqr=vm((2, 2 * z.NS - 1, z.R2, d // 2), BF),
        gqs=vm((2, z.QN, z.R2, z.C4), BF),
        gqf=vm((z.NJ, z.R2, z.C4), BF),
        kgs=vm((z.NJ, z.KR, d), BF),
        kgf=vm((z.NJ, z.KR, d), BF),
        kg2=vm((z.NS, z.KR, z.R), BF),
        kgx=vm((z.NS, z.KR, z.R), BF),
        sv=vm((2, 8, d), F32),
        sva=vm((z.NJ, 8, d), F32),
        svb=vm((z.NS, 8, d), F32),
        sw=vm((2, 24, 128), F32),
        swa=vm((z.NJ, 24, 128), F32),
        swb=vm((z.NS, 24, 128), F32),
        own_mlp=vm((rows, d), F32),
        own_d=vm((rows, d), F32 if z.LEN <= 1024 else BF),
        send=pltpu.SemaphoreType.DMA((48 * z.NS // 2,)),
        recv=pltpu.SemaphoreType.DMA((48 * z.NS // 2,)),
        lsem=pltpu.SemaphoreType.DMA((12,)),
    )


def kernel(z, ins, outs, m):
    x_hbm, g_hbm, lens, pars, wq_hbm, wkv_hbm, wout_hbm, wup_hbm, wdn_hbm, tab_hbm = ins
    o_lo, o_gi, o_up, o_dn, o_wo, o_wq, o_wkv, o_sv, o_sw = outs
    NS, NJ, BS, BJ, SL, SPAN, D, HF = z.NS, z.NJ, z.BS, z.BJ, z.SL, z.SPAN, z.D, z.HF
    ROWS, LEN, QN, R, R2, CW, C4, PG, PR = (
        z.ROWS, z.LEN, z.QN, z.R, z.R2, z.CW, z.C4, z.PG, z.PR,
    )
    links = Links(m.send, m.recv)
    s = lax.axis_index("seq")
    j = lax.axis_index("slot")
    c = bit_of(j, 0)
    ts = bit_of(s, BS - 1)
    rank = lax.div(j, 2)
    buddy = (s, flip(j, 0))
    scale = HEAD**-0.5

    def seq_device(n):
        return (n, j)

    def slot_device(n):
        return (s, n)

    def load(k, src, dst):
        copy = pltpu.make_async_copy(src, dst, m.lsem.at[k])
        copy.start()
        return copy

    load_x = load(0, x_hbm, m.x)
    load_g = load(1, g_hbm, m.g2.at[pl.ds(0, ROWS), :])
    load_tab = load(2, tab_hbm.at[:, pl.ds(pl.multiple_of(s * SPAN, SPAN), SPAN), :], m.tab)
    load_wkv = load(3, wkv_hbm, m.wkv)
    load_wq = load(4, wq_hbm, m.wq)
    load_wout = load(5, wout_hbm, m.wout)
    load_wup = load(6, wup_hbm.at[:, pl.ds(pl.multiple_of(c * HF, HF), HF)], m.wup)
    load_wdn = load(7, wdn_hbm.at[pl.ds(pl.multiple_of(c * HF, HF), HF), :], m.wdn)

    for i in range(SL):
        m.kv[i] = jnp.zeros((NS, SPAN, PAIR), BF)
    near = [seq_device(lax.rem(s + d, NS)) for d in range(1, NS)]
    near += [slot_device(lax.rem(j + d, NJ)) for d in range(1, NJ)]
    near += [(flip(s, BS - 1), flip(j, 0))]
    barrier = pltpu.get_barrier_semaphore()
    for device in near:
        pl.semaphore_signal(barrier, inc=1, device_id=device, device_id_type=MESH)
    pl.semaphore_wait(barrier, len(near))

    spot = s * SPAN + lax.broadcasted_iota(jnp.int32, (SPAN, 1), 0)
    load_x.wait()
    load_g.wait()
    for i in range(SL):
        rows = slice(i * SPAN, (i + 1) * SPAN)
        v = m.x[rows, :].astype(F32)
        v = v - jnp.mean(v, axis=-1, keepdims=True)
        v = v * lax.rsqrt(jnp.mean(v * v, axis=-1, keepdims=True) + 1e-05)
        m.ain[rows, :] = (v * pars[0:1, :] + pars[1:2, :]).astype(BF)
        m.mlp2[rows, :] = (v * pars[2:3, :] + pars[3:4, :]).astype(BF)
        m.g2[rows, :] = jnp.where(spot < lens[i], m.g2[rows, :].astype(F32), 0.0).astype(BF)
    own, theirs = pl.ds(0, ROWS), pl.ds(ROWS, ROWS)
    msend, dsend = m.g2.at[theirs, :], m.act.at[theirs, pl.ds(0, D)]
    mrecv, drecv = m.mlp2.at[own, :], m.mlp2.at[theirs, :]
    got_m = links.copy(m.mlp2.at[own, :], m.mlp2.at[theirs, :], buddy)
    got_g = links.copy(m.g2.at[own, :], m.g2.at[theirs, :], buddy)
    got_m.start()
    got_g.start()

    lane = lax.broadcasted_iota(jnp.int32, (SPAN, PAIR), 1)
    low = lane < HEAD
    load_tab.wait()
    tables = (m.tab[0], m.tab[1], m.tab[2])
    key_tables = (
        jnp.where(low, tables[0], 1.0),
        jnp.where(low, tables[1], 0.0),
        jnp.where(low, tables[2], 0.0),
    )
    load_wkv.wait()
    kv_pre = dot(m.ain[...], m.wkv[...]) + pars[11:12, 0:PAIR]
    for i in range(SL):
        m.kv[i, s] = turned(kv_pre[i * SPAN : (i + 1) * SPAN, :], key_tables).astype(BF)
    gather = []
    for d in range(1, NS):
        up_to = lax.rem(s + d, NS)
        copy = links.copy(m.kv.at[:, s], m.kv.at[:, s], seq_device(up_to))
        sends = s + d < NS
        gets = s - d >= 0
        gather.append((copy, sends, gets))

        @pl.when(sends)
        def _(copy=copy):
            copy.start()

        links.waits.append((sends, copy))

    load_wq.wait()
    load_wout.wait()
    for i in range(SL):
        rows = slice(i * SPAN, (i + 1) * SPAN)
        q_pre = dot(m.ain[rows, :], m.wq[...]) + pars[4:5, :]
        back = dot(m.g2[rows, :], m.wout[...], 1, 1)
        for p in range(z.PAIRS):
            hg, at = p // PG, (p % PG) * SPAN
            cols = slice(p * PAIR, (p + 1) * PAIR)
            q = turned(q_pre[:, cols], tables)
            a = back[:, cols]
            m.l1[hg, i, at : at + SPAN, :] = jnp.where(low, q, 0.0).astype(BF)
            m.l2[hg, i, PR + at : PR + at + SPAN, :] = jnp.where(low, 0.0, q).astype(BF)
            m.l2[hg, i, at : at + SPAN, :] = jnp.where(low, a, 0.0).astype(BF)
            m.l1[hg, i, PR + at : PR + at + SPAN, :] = jnp.where(low, 0.0, a).astype(BF)

    load_wup.wait()
    load_wdn.wait()
    m.sv[0] = jnp.zeros((8, D), F32)
    low_bits = list(range(BS - 1))
    turned_bits = low_bits[1:] + low_bits[:1]
    seq_stage = lambda b: (bit_of(s, b), (flip(s, b), j))
    slot_stage = lambda b: (bit_of(j, b), (s, flip(j, b)))
    dn_first = [
        [
            Halving(
                links,
                m.dn.at[k, p],
                [slot_stage(b) for b in range(BJ - 1, 0, -1)],
                m.dnr.at[k, p],
            )
            for p in range(2)
        ]
        for k in range(z.CH)
    ]
    up_order = [(low_bits if k % 2 == 0 else turned_bits) + [BS - 1] for k in range(z.CH)]
    ups = [
        Halving(links, m.up.at[k], [seq_stage(b) for b in up_order[k]], m.upr.at[k])
        for k in range(z.CH)
    ]

    RB = 256

    def bias_of(at):
        row, col = at // D, at % D
        if col + CW <= D:
            return pars[7 + row : 8 + row, col : col + CW]
        return jnp.concatenate(
            [pars[7 + row : 8 + row, col:], pars[8 + row : 9 + row, : col + CW - D]], axis=1
        )

    def feed(k, first, last):
        cols = slice(k * CW, (k + 1) * CW)
        bias = jnp.where(c == 0, bias_of(k * CW), bias_of(k * CW + HF))

        def block(i, total):
            rows = pl.ds(pl.multiple_of(i * RB, RB), RB)
            up = dot(m.mlp2[rows, :], m.wup[:, cols]) + bias
            back = dot(m.g2[rows, :], m.wdn[cols, :], 1, 1)
            a, slope = gelu_pair(up)
            back = back * slope
            m.act[rows, cols] = a.astype(BF)
            m.dup[rows, cols] = back.astype(BF)
            return total + jnp.sum(back, axis=0, keepdims=True)

        return lax.fori_loop(first, last, block, jnp.zeros((1, CW), F32))

    def feed_grads(k):
        cols = slice(k * CW, (k + 1) * CW)
        part = dot(m.act[:, cols], m.g2[...], 0, 0).astype(BF)
        for p in range(2):
            for q in range(QN):
                m.dn[k, p, q] = part[p * z.FRH : (p + 1) * z.FRH, q * z.DW : (q + 1) * z.DW]
            dn_first[k][p].start(0)
        part = dot(m.mlp2[...], m.dup[:, cols], 0, 0).astype(BF)
        for n in range(NS):
            m.up[k, placed(n, up_order[k])] = part[n * R : (n + 1) * R, :]
        ups[k].start(0)

    halfway = ROWS // RB
    totals = []
    for k in range(z.CH):
        total = feed(k, 0, halfway)
        if k == 0:
            got_m.wait()
            got_g.wait()
        totals.append(total + feed(k, halfway, 2 * halfway))
        feed_grads(k)
    total = jnp.concatenate(totals, axis=1)
    for q in range(z.FF // D):
        piece = total[:, (q * D) % HF : (q * D) % HF + D]
        m.sv[0, q : q + 1, :] = jnp.where(c == (q * D) // HF, piece, 0.0)

    kept = rank
    dn_levels, at = [], 0
    for l in range(BS - 1):
        level = []
        for n in range(z.CH >> (l + 1)):
            base = n * 2 ** (l + 1) + lax.rem(s, 2**l)
            mine = bit_of(s, l)
            keep = base + mine * 2**l
            give = base + (1 - mine) * 2**l
            for p in range(2):
                copy = links.copy(m.dn.at[give, p, kept], m.dnr2.at[at], (flip(s, l), j))
                level.append((copy, keep, p, at, n))
                at += 1
        dn_levels.append(level)

    def dn_start(l, n):
        for copy, keep, p, at, group in dn_levels[l]:
            if group == n:
                copy.start()
                links.waits.append(copy)

    def dn_finish(l, n):
        for copy, keep, p, at, group in dn_levels[l]:
            if group == n:
                copy.wait_recv()
                m.dn[keep, p, kept] = m.dn[keep, p, kept] + m.dnr2[at]

    dn_arrivals = links.take(4)

    def dn_last():
        mine = lax.rem(s, z.CH)
        for p in range(2):
            part = m.dn[mine, p, kept]
            for h in range(2):
                m.dnm[2 * p + h] = part[:, h * (z.DW // 2) : (h + 1) * (z.DW // 2)]
                links.unless(
                    jnp.logical_and(ts == c, c == h),
                    m.dnm.at[2 * p + h],
                    m.dnf.at[p, ts],
                    (put(s, BS - 1, c), put(j, 0, h)),
                    dn_arrivals + 2 * p + ts,
                )()

    up_arrivals = links.take(z.CPP * QN)

    def up_end(k):
        piece, n = (k * CW) // z.W, k % z.CPP
        target = c * QN + piece
        return links.unless(
            target == j,
            m.up.at[k, ups[k].end],
            m.upf.at[n, rank],
            (s, target),
            up_arrivals + n * QN + rank,
        )

    up_last = [up_end(k) for k in range(z.CH)]

    dkvs = [
        Halving(links, m.dks.at[i], [seq_stage(b) for b in range(BS)], m.dkr.at[i])
        for i in range(SL)
    ]
    pos = [placed(n, list(range(BS))) for n in range(NS)]
    coef = scale * math.log2(math.e)
    key_spot = lax.broadcasted_iota(jnp.int32, (SPAN, LEN), 1)
    row_spot = s * SPAN + lax.broadcasted_iota(jnp.int32, (SPAN, LEN), 0)

    def attend(hg, i):
        kv = m.kv[i].reshape(LEN, PAIR)
        m.kvs[...] = kv
        m.vks[...] = pltpu.roll(kv.astype(F32), HEAD, 1).astype(BF)
        length = jnp.int32(0)
        for n in range(SL):
            length = jnp.where(i == n, lens[n], length)
        allowed = jnp.logical_and(key_spot <= row_spot, key_spot < length)
        m.bias[...] = jnp.where(allowed, 0.0, -1e9)
        sides = (m.kvs, m.vks)
        rows = pl.ds(pl.multiple_of(i * SPAN, SPAN), SPAN)
        step = z.STEP
        d_key = d_value = None
        for first in range(0, PG, step):
            count = step * SPAN
            even = slice(first * SPAN, first * SPAN + count)
            odd = slice(PR + first * SPAN, PR + first * SPAN + count)
            halves = (slice(0, count), slice(count, 2 * count))
            q = (m.l1[hg, i, even, :], m.l2[hg, i, odd, :])
            a = (m.l2[hg, i, even, :], m.l1[hg, i, odd, :])
            mask = jnp.concatenate([m.bias[...]] * step, axis=0)
            mixed, dqs = {}, {}
            for group in ((0, 1),) if LEN <= 1024 else ((0,), (1,)):
                raw = {e: dot(q[e], sides[e][...], 1, 1) for e in group}
                dps = {e: dot(a[e], sides[1 - e][...], 1, 1) for e in group}
                probs = {}
                for e in group:
                    score = raw[e] * coef + mask
                    w = jnp.exp2(score - jnp.max(score, axis=-1, keepdims=True))
                    probs[e] = w * (1.0 / jnp.sum(w, axis=-1, keepdims=True))
                for e in group:
                    rounded = probs[e].astype(BF)
                    mixed[e] = dot(rounded, sides[1 - e][...])
                    (m.r2 if e == 0 else m.r1)[halves[e], :] = rounded
                for e in group:
                    pd = probs[e] * dps[e]
                    ds = (pd - probs[e] * jnp.sum(pd, axis=-1, keepdims=True)).astype(BF)
                    (m.r1 if e == 0 else m.r2)[halves[e], :] = ds
                    dqs[e] = dot(ds, sides[e][...])
            for p in range(step):
                at = slice(p * SPAN, (p + 1) * SPAN)
                n = hg * PG + first + p
                cols = slice(n * PAIR, (n + 1) * PAIR)
                m.att[rows, cols] = jnp.where(low, mixed[0][at], mixed[1][at]).astype(BF)
                dq = jnp.where(low, dqs[0][at], dqs[1][at]) * scale
                m.dq[rows, cols] = turned_back(dq, tables).astype(BF)
            if step == PG:
                one = dot(m.l1[hg, i], m.r1[...], 0, 0)
                two = dot(m.l2[hg, i], m.r2[...], 0, 0)
            else:
                one = dot(m.l1[hg, i, even, :], m.r1[halves[0], :], 0, 0)
                one = one + dot(m.l1[hg, i, odd, :], m.r1[halves[1], :], 0, 0)
                two = dot(m.l2[hg, i, even, :], m.r2[halves[0], :], 0, 0)
                two = two + dot(m.l2[hg, i, odd, :], m.r2[halves[1], :], 0, 0)
            key_part = one[:HEAD] + two[HEAD:]
            value_part = one[HEAD:] + two[:HEAD]
            d_key = key_part if d_key is None else d_key + key_part
            d_value = value_part if d_value is None else d_value + value_part
        d_key = d_key * scale
        return jnp.concatenate([d_key, d_value], axis=0)

    def hooked(hooks, i):
        for n, steps in hooks.items():

            @pl.when(i == n)
            def _(steps=steps):
                for step in steps:
                    step()

    kv_in = []
    for copy, sends, gets in gather:

        @pl.when(gets)
        def _(copy=copy):
            copy.wait_recv()

    def up_step(k, n):
        return lambda: ups[k].step(n)

    def dn_y(k):
        def go():
            for p in range(2):
                for n in range(BJ - 1):
                    dn_first[k][p].finish(n)
                    if n + 1 < BJ - 1:
                        dn_first[k][p].start(n + 1)

        return go

    early = {n: [] for n in range(SL)}
    late = {n: [] for n in range(SL)}
    tail = []
    plan = [early[n] for n in range(SL)] + [late[n] for n in range(SL)] + [tail]

    def at_point(n, step):
        plan[min(n, 2 * SL)].append(step)

    for k in range(z.CH):
        for n in range(1, BS + 1):
            at_point(k // 2 + 2 * (n - 1) if BS == 3 else 2 * SL, up_step(k, n))
        at_point(k // 2 + 2 * BS - 2 if BS == 3 else 2 * SL, lambda k=k: up_last[k]())
    for k in range(z.CH):
        at_point(1 + k if BS == 3 else 2 * SL, dn_y(k))
        if k % 2 == 1:
            at_point(1 + k if BS == 3 else 2 * SL, lambda k=k: dn_start(0, k // 2))
    for l in range(BS - 1):
        for n in range(z.CH >> (l + 1)):
            point = (5 + 2 * n if l == 0 else 8) if BS == 3 else 2 * SL
            at_point(point, lambda l=l, n=n: dn_finish(l, n))
            if l + 1 < BS - 1 and n % 2 == 1:
                at_point(point, lambda l=l, n=n: dn_start(l + 1, n // 2))
    at_point(2 * SL, dn_last)

    def early_body(i, _):
        m.dkt[i] = attend(0, i).astype(m.dkt.dtype)
        hooked(early, i)
        return 0

    lax.fori_loop(0, SL, early_body, 0)

    wo_order = [turned_bits, low_bits]
    wo_pipes = [
        Halving(
            links,
            m.wo.at[hg],
            [slot_stage(0)] + [seq_stage(b) for b in wo_order[hg]],
            m.wor.at[hg],
        )
        for hg in range(2)
    ]
    gq_order = [low_bits + [BS - 1], turned_bits + [BS - 1]]
    gq_pipes = [
        Halving(
            links,
            m.gq.at[hg],
            [slot_stage(0)] + [seq_stage(b) for b in gq_order[hg]],
            m.gqr.at[hg],
        )
        for hg in range(2)
    ]
    gq_arrivals = links.take(NJ)

    def project(hg):
        cols = slice(hg * (D // 2), (hg + 1) * (D // 2))
        part = dot(m.att[:, cols], m.g2[0:ROWS, :], 0, 0).astype(BF)
        for n in range(NS // 2):
            for r in range(2):
                at = n * R + r * R2
                m.wo[hg, r * (NS // 2) + placed(n, wo_order[hg])] = part[at : at + R2, :]
        wo_pipes[hg].start(0)
        part = dot(m.ain[...], m.dq[:, cols], 0, 0).astype(BF)
        for n in range(NS):
            for r in range(2):
                at = n * R + r * R2
                m.gq[hg, r * NS + placed(n, gq_order[hg])] = part[at : at + R2, :]
        gq_pipes[hg].start(0)

    wo_direct = [
        Direct(links, NJ, j, slot_device, lambda n, hg=hg: m.wos.at[hg, n], m.wof.at[hg])
        for hg in range(2)
    ]

    def wo_last(hg):
        part = m.wo[hg, wo_pipes[hg].end]
        for n in range(NJ):
            m.wos[hg, n] = part[:, n * C4 : (n + 1) * C4]
        m.wof[hg, j] = m.wos[hg, j]
        wo_direct[hg].start()

    def wo_sum(hg):
        wo_direct[hg].finish()
        for r in range(2):
            total = m.wof[hg, r].astype(F32)
            for n in range(1, QN):
                total = total + m.wof[hg, 2 * n + r].astype(F32)
            m.wox[hg, r] = total

    def gq_last(hg):
        part = m.gq[hg, gq_pipes[hg].end]
        for n in range(QN):
            m.gqs[hg, n] = part[:, n * C4 : (n + 1) * C4]
            target = hg * QN + n
            links.unless(
                target == j, m.gqs.at[hg, n], m.gqf.at[j], (s, target), gq_arrivals + j
            )()

    project(0)
    small = BS == 3
    if small:
        late[0] += [lambda: wo_pipes[0].step(1), lambda: gq_pipes[0].step(1)]
        late[2] += [lambda: wo_pipes[0].step(2), lambda: gq_pipes[0].step(2)]
        late[3] += [lambda: wo_pipes[0].step(3), lambda: gq_pipes[0].step(3)]
        late[3] += [lambda: wo_last(0)]
        tail += [lambda: gq_pipes[0].step(4), lambda: gq_last(0)]
    else:
        for n in range(1, BS + 1):
            tail += [lambda n=n: wo_pipes[0].step(n)]
        tail += [lambda: wo_last(0)]
        for n in range(1, BS + 2):
            tail += [lambda n=n: gq_pipes[0].step(n)]
        tail += [lambda: gq_last(0)]
    for i in range(SL):
        for n in range(1, BS + 1):
            if i + n < SL:
                late[i + n] += [lambda i=i, n=n: dkvs[i].step(n)]

    def late_body(i, _):
        total = (m.dkt[i] + attend(1, i)).astype(BF)
        for n in range(NS):
            m.dks[i, pos[n]] = total[:, n * SPAN : (n + 1) * SPAN]
        for n in range(SL):

            @pl.when(i == n)
            def _(n=n):
                dkvs[n].start(0)

        hooked(late, i)
        return 0

    lax.fori_loop(0, SL, late_body, 0)

    left = []
    for i in range(SL):
        for n in range(1, BS + 1):
            if i + n >= SL:
                left.append((i + n - SL, lambda i=i, n=n: dkvs[i].step(n)))

    def dkv_round(r):
        for at, step in left:
            if at == r:
                step()

    project(1)
    dkv_round(0)
    for step in tail:
        step()
    for k in range(halfway):
        rows = slice(ROWS + k * RB, ROWS + (k + 1) * RB)
        here = slice(k * RB, (k + 1) * RB)
        msend[here, :] = dot(m.act[rows, :], m.wdn[...]).astype(BF)
    for k in range(halfway):
        rows = slice(ROWS + k * RB, ROWS + (k + 1) * RB)
        here = slice(k * RB, (k + 1) * RB)
        dsend[here, :] = dot(m.dup[rows, :], m.wup[...], 1, 1).astype(BF)
    got_out = links.start(msend, mrecv, buddy)
    got_back = links.start(dsend, drecv, buddy)
    wo_pipes[1].step(1)
    gq_pipes[1].step(1)
    dkv_round(1)
    for k in range(halfway):
        here = slice(k * RB, (k + 1) * RB)
        m.own_mlp[here, :] = dot(m.act[here, :], m.wdn[...]) + dot(m.att[here, :], m.wout[...])
        m.own_d[here, :] = dot(m.dup[here, :], m.wup[...], 1, 1).astype(m.own_d.dtype)
    got_out.wait_recv()
    got_back.wait_recv()
    dkv_round(2)
    for step in range(2, BS + 1):
        wo_pipes[1].step(step)
        gq_pipes[1].step(step)
    wo_last(1)

    def normed(rows):
        v = m.x[rows, :].astype(F32)
        v = v - jnp.mean(v, axis=-1, keepdims=True)
        inv = lax.rsqrt(jnp.mean(v * v, axis=-1, keepdims=True) + 1e-05)
        return v * inv, inv

    g_sum = jnp.zeros((1, D), F32)
    gain_two = jnp.zeros((1, D), F32)
    shift_two = jnp.zeros((1, D), F32)
    out_copies = []
    for i in range(SL):
        rows = slice(i * SPAN, (i + 1) * SPAN)
        total = m.x[rows, :].astype(F32) + m.own_mlp[rows, :] + mrecv[rows, :].astype(F32)
        total = total + (pars[5:6, :] + pars[6:7, :])
        mrecv[rows, :] = jnp.where(spot < lens[i], total, 0.0).astype(BF)
        d_mlp = m.own_d[rows, :] + drecv[rows, :].astype(F32)
        unit, _ = normed(rows)
        gain_two = gain_two + jnp.sum(d_mlp * unit, axis=0, keepdims=True)
        shift_two = shift_two + jnp.sum(d_mlp, axis=0, keepdims=True)
        m.own_d[rows, :] = (d_mlp * pars[2:3, :]).astype(m.own_d.dtype)
        g_sum = g_sum + jnp.sum(m.g2[rows, :].astype(F32), axis=0, keepdims=True)
    copy = pltpu.make_async_copy(mrecv, o_lo, m.lsem.at[8])
    copy.start()
    out_copies.append(copy)
    m.sv[0, 4:5, :] = gain_two
    m.sv[0, 5:6, :] = shift_two
    m.sv[0, 6:7, :] = g_sum
    sv_one = Direct(links, NJ, j, slot_device, lambda n: m.sv.at[0], m.sva)
    sv_two = Direct(links, NS, s, seq_device, lambda n: m.sv.at[1], m.svb)
    m.sva[j] = m.sv[0]
    sv_one.start()

    dkv_round(3)
    gq_pipes[1].step(BS + 1)
    gq_last(1)

    bkv = jnp.zeros((1, PAIR), F32)
    for i in range(SL):
        d_kv = jnp.transpose(m.dks[i, dkvs[i].end].astype(F32))
        d_kv = turned_back(d_kv, key_tables)
        bkv = bkv + jnp.sum(d_kv, axis=0, keepdims=True)
        m.kvs[i * SPAN : (i + 1) * SPAN, :] = d_kv.astype(BF)
    d_kv_pre = m.kvs[0:ROWS, :]
    part = dot(d_kv_pre, m.ain[...], 0, 0).astype(BF)
    for n in range(NJ):
        m.kgs[n] = part[n * z.KR : (n + 1) * z.KR, :]
    kg_one = Direct(links, NJ, j, slot_device, lambda n: m.kgs.at[n], m.kgf)
    kg_two = Direct(links, NS, s, seq_device, lambda n: m.kg2.at[n], m.kgx)
    m.kgf[j] = m.kgs[j]
    kg_one.start()

    gain_one = jnp.zeros((1, D), F32)
    shift_one = jnp.zeros((1, D), F32)
    bq = jnp.zeros((1, D), F32)
    for i in range(SL):
        rows = slice(i * SPAN, (i + 1) * SPAN)
        dq = m.dq[rows, :]
        bq = bq + jnp.sum(dq.astype(F32), axis=0, keepdims=True)
        d_in = dot(dq, m.wq[...], 1, 1) + dot(m.kvs[rows, :], m.wkv[...], 1, 1)
        unit, inv = normed(rows)
        gain_one = gain_one + jnp.sum(d_in * unit, axis=0, keepdims=True)
        shift_one = shift_one + jnp.sum(d_in, axis=0, keepdims=True)
        d_unit = d_in * pars[0:1, :] + m.own_d[rows, :]
        along = jnp.mean(d_unit * unit, axis=-1, keepdims=True)
        d_unit = d_unit - jnp.mean(d_unit, axis=-1, keepdims=True) - unit * along
        m.own_mlp[rows, :] = m.g2[rows, :].astype(F32) + d_unit * inv
    copy = pltpu.make_async_copy(m.own_mlp, o_gi, m.lsem.at[9])
    copy.start()
    out_copies.append(copy)
    m.sw[0] = jnp.zeros((24, 128), F32)
    for n in range(D // 128):
        cols = slice(n * 128, (n + 1) * 128)
        m.sw[0, n : n + 1, :] = gain_one[:, cols]
        m.sw[0, 6 + n : 7 + n, :] = shift_one[:, cols]
        m.sw[0, 12 + n : 13 + n, :] = bq[:, cols]
    m.sw[0, 18:19, :] = bkv
    sw_one = Direct(links, NJ, j, slot_device, lambda n: m.sw.at[0], m.swa)
    sw_two = Direct(links, NS, s, seq_device, lambda n: m.sw.at[1], m.swb)
    m.swa[j] = m.sw[0]
    sw_one.start()

    def summed(ref, size):
        total = ref[0].astype(F32)
        for n in range(1, size):
            total = total + ref[n].astype(F32)
        return total

    sv_one.finish()
    m.sv[1] = summed(m.sva, NJ)
    m.svb[s] = m.sv[1]
    sv_two.start()
    kg_one.finish()
    part = summed(m.kgf, NJ).astype(BF)
    for n in range(NS):
        m.kg2[n] = part[:, n * R : (n + 1) * R]
    m.kgx[s] = m.kg2[s]
    kg_two.start()
    sw_one.finish()
    m.sw[1] = summed(m.swa, NJ)
    m.swb[s] = m.sw[1]
    sw_two.start()

    wo_sum(0)
    wo_sum(1)
    for r in range(2):
        m.woy[0, r] = m.wox[1 - ts, r].astype(BF)
    wo_end = links.start(m.woy.at[0], m.woy.at[1], (flip(s, BS - 1), j))

    for n in range(z.CPP):
        for r in range(QN):
            links.arrived(m.upf.at[n, r], up_arrivals + n * QN + r)
        o_up[:, n * CW : (n + 1) * CW] = summed(m.upf.at[n], QN)
    for p in range(2):
        for t in range(2):
            links.arrived(m.dnf.at[p, t], dn_arrivals + 2 * p + t)
        o_dn[p * z.FRH : (p + 1) * z.FRH, :] = summed(m.dnf.at[p], 2)
    for n in range(NJ):
        links.arrived(m.gqf.at[n], gq_arrivals + n)
    for r in range(2):
        total = m.gqf[r].astype(F32)
        for n in range(1, QN):
            total = total + m.gqf[2 * n + r].astype(F32)
        o_wq[r * R2 : (r + 1) * R2, :] = total
    wo_end.wait_recv()
    for r in range(2):
        o_wo[r * R2 : (r + 1) * R2, :] = m.wox[ts, r] + m.woy[1, r].astype(F32)
    sv_two.finish()
    o_sv[...] = summed(m.svb, NS)
    kg_two.finish()
    o_wkv[...] = jnp.transpose(summed(m.kgx, NS))
    sw_two.finish()
    o_sw[...] = summed(m.swb, NS)
    for copy in out_copies:
        copy.wait()
    links.finish()


class Names:
    pass


def body(
    hidden_in, lengths, out_grad, ln1_gain, ln1_bias, ln2_gain, ln2_bias, w_query, b_query,
    w_keyval, b_keyval, w_out, b_out, w_up, b_up, w_down, b_down,
):
    SL, SPAN, D = hidden_in.shape
    FF = w_up.shape[1]
    z = Sizes(lax.axis_size("seq"), lax.axis_size("slot"), SL, SPAN, D, FF)
    pad = jnp.zeros((D - b_keyval.shape[0],), BF)
    pars = jnp.concatenate(
        [ln1_gain, ln1_bias, ln2_gain, ln2_bias, b_query, b_out, b_down, b_up, b_keyval, pad]
    )
    pars = pars.astype(F32).reshape(8 + FF // D, D)
    scratch = scratch_of(z)
    names = list(scratch)
    n_in, n_out = 10, 9

    def call(*refs):
        m = Names()
        for name, ref in zip(names, refs[n_in + n_out :]):
            setattr(m, name, ref)
        kernel(z, refs[:n_in], refs[n_in : n_in + n_out], m)

    anywhere = pl.BlockSpec(memory_space=pl.ANY)
    vmem = pl.BlockSpec(memory_space=pltpu.VMEM)
    shape = jax.ShapeDtypeStruct
    lo, gi, up, dn, wo, wq, wkv, sv, sw = pl.pallas_call(
        call,
        out_shape=[
            shape((z.ROWS, D), BF),
            shape((z.ROWS, D), F32),
            shape((z.R, z.W), F32),
            shape((z.CW, z.DW // 2), F32),
            shape((z.R, z.C4), F32),
            shape((z.R, z.C4), F32),
            shape((z.R, z.KR), F32),
            shape((8, D), F32),
            shape((24, 128), F32),
        ],
        in_specs=[
            anywhere,
            anywhere,
            pl.BlockSpec(memory_space=pltpu.SMEM),
            vmem,
            anywhere,
            anywhere,
            anywhere,
            anywhere,
            anywhere,
            anywhere,
        ],
        out_specs=[anywhere, anywhere] + [vmem] * 7,
        scratch_shapes=list(scratch.values()),
        compiler_params=pltpu.CompilerParams(
            collective_id=0, has_side_effects=True, vmem_limit_bytes=62 * 2**20
        ),
    )(
        hidden_in.reshape(z.ROWS, D),
        out_grad.reshape(z.ROWS, D),
        lengths,
        pars,
        w_query,
        w_keyval,
        w_out,
        w_up,
        w_down,
        jnp.asarray(rotary_tables(z.LEN)),
    )
    flat = sw.reshape(-1)
    b_down_grad = sv[6]
    return (
        lo.reshape(hidden_in.shape),
        gi.reshape(hidden_in.shape),
        flat[0:D],
        flat[D : 2 * D],
        sv[4],
        sv[5],
        wq,
        flat[2 * D : 3 * D],
        wkv,
        flat[3 * D : 3 * D + 2 * HEAD],
        wo,
        b_down_grad,
        up,
        sv[: FF // D].reshape(FF),
        dn,
        b_down_grad,
    )


def solution(mesh):
    rows, whole, cut = P("slot", "seq", None), P(), P("seq", "slot")
    return jax.shard_map(
        body,
        mesh=mesh,
        in_specs=(rows, P("slot"), rows) + (whole,) * 14,
        out_specs=(
            rows, rows, whole, whole, whole, whole, cut, whole, cut, whole, cut, whole, cut, whole,
            cut, whole,
        ),
        check_vma=False,
    )
```

time: 897 us -> 151 us (0.17)
  waiting for transfers between devices: 614 us -> 0 us
  Pallas kernels: 0 us -> 126 us
  matrix products: 115 us -> 0 us
  other arithmetic: 59.7 us -> 0.01 us
  blocking collectives: 41.3 us -> 0 us
  local copies, waits for them, and re-layouts: 45.2 us -> 23.2 us
  between operations: 15.3 us -> 0.69 us
    reduce_scatter x7 -> x0, waiting for transfers between devices: 556 us -> none  [the longest x1 164 us: body(): lax.psum_scatter(grad_w_up, 'seq', scatter_dimension=0, tiled=True)]
    pallas_call x0 -> x1, Pallas kernels: none -> 126 us  [body(): pl.pallas_call(call, out_shape=[shape((z.ROWS, D), BF), shape((z.ROWS, D)...]
    dot_general x43 -> x0, matrix products: 115 us -> none  [the longest x4 10.7 us: backward_slot(): jnp.einsum('chd,kd->hck', d_slot, kv_slot[:, HEAD:], preferred_element_ty...]
    psum x1 -> x0, blocking collectives: 41.3 us -> none  [body(): lax.psum((grad_gain_one, grad_shift_one, grad_gain_two, grad_shift_two, g...]
    unnamed x16 -> x0, waiting for transfers between devices: 28.9 us -> none
    all_gather x1 -> x0, waiting for transfers between devices: 28.6 us -> none  [body(): kv_whole = lax.all_gather(kv_local, 'seq', axis=1, tiled=True)]
    convert_element_type x16 -> x0, other arithmetic: 27.5 us -> none  [the longest x1 16.8 us: body(): act = act32.astype(jnp.bfloat16)]
    reduce_sum x10 -> x0, other arithmetic: 14.2 us -> none  [the longest x4 5.08 us: forward_slot(): summed = jnp.sum(weights, axis=-1, keepdims=True)]
  transfers between devices with their start and end apart: 12 -> 0, of which waited for: 9 -> 0; matrix products, arithmetic and copies ran while one was open for 13% -> 0% of each run, Pallas kernels for 0% -> 0%
where the time goes in v2:
time: 151 us; the launch traced here: 150 us
  Pallas kernels  126 us (83%)
  local copies, waits for them, and re-layouts  23.2 us (15%)
    pallas_call x1, Pallas kernels, body(): pl.pallas_call(call, out_shape=[shape((z.ROWS, D), BF), shape((z.ROWS, D)...  126 us
    unnamed x27, local copies, waits for them, and re-layouts  16.8 us

profile of v2, /device:TPU:0, one launch (start us, length us, event | category | flops | bytes accessed | tf_op | source)
XLA Modules:
  0.0 150.3 jit_solution(17822121336007535946)
XLA Ops:
  0.7 0.9 dynamic-update-slice
  1.5 0.8 dynamic-update-slice.1
  2.4 0.9 dynamic-update-slice.2
  3.2 0.9 dynamic-update-slice.3
  4.1 0.9 dynamic-update-slice.4
  4.9 0.8 dynamic-update-slice.5
  5.8 0.9 dynamic-update-slice.6
  6.6 0.9 dynamic-update-slice.7
  7.5 0.8 dynamic-update-slice.8
  8.3 0.2 dynamic-update-slice.9
  8.5 0.7 reshape.61.refs_3_
  9.2 126.5 %shard_map.297 = (bf16[512,768]{1,0:T(8,128)(2,1)}, f32[512,768]{1,0:T(8,128)}, f32[96,768]{1,0:T(8,128)}, f32[384,192]{1,0:T(8,128)}, f32[96,192]{1,0:T(8,128)}...) custom-call(bf16[512,768]{1,0:T(8,128)(2,1)} %bitcast.14, ...), custom_call_target="tpu_custom_call" | custom-call | tf_op jit(solution)/shard_map/pallas_call | solution.py:956
  135.7 0.0 copy-start
  135.7 1.3 slice_bitcast_fusion.3
  137.0 1.4 slice_bitcast_fusion
  138.3 0.7 slice.47
  139.1 1.5 slice_reduce_fusion
  140.6 0.0 copy-start.4
  140.6 0.6 reshape.60
  141.2 1.5 copy.34
  142.7 1.9 %copy.35 = f32[384,192]{0,1:T(8,128)} copy(f32[384,192]{1,0:T(8,128)} %get-tuple-element.48) | data formatting | bytes 589824
  144.5 0.6 copy.52
  145.1 2.1 %copy.53 = bf16[4,128,768]{2,1,0:T(8,128)(2,1)} copy(bf16[4,128,768]{2,1,0:T(8,128)(2,1)} %bitcast.13) | data formatting | bytes 1572864
  147.2 0.0 copy-done
  147.2 0.0 copy-start.3
  147.2 0.0 copy-start.2
  147.2 0.0 copy-start.1
  147.2 1.1 copy.54
  148.3 0.0 copy-done.4
  148.3 0.0 copy-done.3
  148.3 0.6 copy.55
  149.0 0.0 copy-done.2
  149.0 0.6 copy.56
  149.6 0.0 copy-done.1
  149.6 0.7 copy.57
  (2 shorter events, 0.0 us)
Async XLA Ops:
  135.7 11.5 %copy-start = (f32[512,768]{1,0:T(8,128)S(1)}, f32[512,768]{1,0:T(8,128)}, u32[]{:S(2)}) copy-start(f32[512,768]{1,0:T(8,128)} %get-tuple-element.26) | copy-start | bytes 4718596
  140.6 7.8 %copy-start.4 = (f32[768]{0:T(1024)}, f32[768]{0:T(1024)S(1)}, u32[]{:S(2)}) copy-start(f32[768]{0:T(1024)S(1)} %get-tuple-element.115) | copy-start | bytes 9220
  147.2 1.2 copy-start.3
  147.2 1.8 %copy-start.2 = (f32[96,192]{1,0:T(8,128)S(1)}, f32[96,192]{1,0:T(8,128)}, u32[]{:S(2)}) copy-start(f32[96,192]{1,0:T(8,128)} %get-tuple-element.114) | copy-start | bytes 221188
  147.2 2.4 %copy-start.1 = (f32[96,768]{1,0:T(8,128)S(1)}, f32[96,768]{1,0:T(8,128)}, u32[]{:S(2)}) copy-start(f32[96,768]{1,0:T(8,128)} %get-tuple-element.116) | copy-start | bytes 884740

commit v3 on v2

--- a/solution.py
+++ b/solution.py
@@ -213,6 +213,7 @@
     vm = pltpu.VMEM
     rows, d = z.ROWS, z.D
     return dict(
+        pars=vm((8 + z.FF // d, d), F32),
         x=vm((rows, d), BF),
         g2=vm((2 * rows, d), BF),
         mlp2=vm((2 * rows, d), BF),
@@ -275,7 +276,9 @@
 
 
 def kernel(z, ins, outs, m):
-    x_hbm, g_hbm, lens, pars, wq_hbm, wkv_hbm, wout_hbm, wup_hbm, wdn_hbm, tab_hbm = ins
+    x_hbm, g_hbm, lens = ins[:3]
+    wq_hbm, wkv_hbm, wout_hbm, wup_hbm, wdn_hbm, tab_hbm = ins[3:9]
+    vectors = ins[9:]
     o_lo, o_gi, o_up, o_dn, o_wo, o_wq, o_wkv, o_sv, o_sw = outs
     NS, NJ, BS, BJ, SL, SPAN, D, HF = z.NS, z.NJ, z.BS, z.BJ, z.SL, z.SPAN, z.D, z.HF
     ROWS, LEN, QN, R, R2, CW, C4, PG, PR = (
@@ -318,8 +321,14 @@
     barrier = pltpu.get_barrier_semaphore()
     for device in near:
         pl.semaphore_signal(barrier, inc=1, device_id=device, device_id_type=MESH)
-    pl.semaphore_wait(barrier, len(near))
-
+
+    pars = m.pars
+    for n, vector in enumerate(vectors[:7]):
+        pars[n : n + 1, :] = vector[...].astype(F32).reshape(1, D)
+    wide = vectors[7][...].astype(F32).reshape(1, z.FF)
+    for n in range(z.FF // D):
+        pars[7 + n : 8 + n, :] = wide[:, n * D : (n + 1) * D]
+    b_keyval = vectors[8][...].astype(F32).reshape(1, PAIR)
     spot = s * SPAN + lax.broadcasted_iota(jnp.int32, (SPAN, 1), 0)
     load_x.wait()
     load_g.wait()
@@ -336,8 +345,6 @@
     mrecv, drecv = m.mlp2.at[own, :], m.mlp2.at[theirs, :]
     got_m = links.copy(m.mlp2.at[own, :], m.mlp2.at[theirs, :], buddy)
     got_g = links.copy(m.g2.at[own, :], m.g2.at[theirs, :], buddy)
-    got_m.start()
-    got_g.start()
 
     lane = lax.broadcasted_iota(jnp.int32, (SPAN, PAIR), 1)
     low = lane < HEAD
@@ -349,9 +356,12 @@
         jnp.where(low, tables[2], 0.0),
     )
     load_wkv.wait()
-    kv_pre = dot(m.ain[...], m.wkv[...]) + pars[11:12, 0:PAIR]
+    kv_pre = dot(m.ain[...], m.wkv[...]) + b_keyval
     for i in range(SL):
         m.kv[i, s] = turned(kv_pre[i * SPAN : (i + 1) * SPAN, :], key_tables).astype(BF)
+    pl.semaphore_wait(barrier, len(near))
+    got_m.start()
+    got_g.start()
     gather = []
     for d in range(1, NS):
         up_to = lax.rem(s + d, NS)
@@ -916,7 +926,7 @@
     sv_two.finish()
     o_sv[...] = summed(m.svb, NS)
     kg_two.finish()
-    o_wkv[...] = jnp.transpose(summed(m.kgx, NS))
+    o_wkv[...] = summed(m.kgx, NS)
     sw_two.finish()
     o_sw[...] = summed(m.swb, NS)
     for copy in out_copies:
@@ -935,14 +945,9 @@
     SL, SPAN, D = hidden_in.shape
     FF = w_up.shape[1]
     z = Sizes(lax.axis_size("seq"), lax.axis_size("slot"), SL, SPAN, D, FF)
-    pad = jnp.zeros((D - b_keyval.shape[0],), BF)
-    pars = jnp.concatenate(
-        [ln1_gain, ln1_bias, ln2_gain, ln2_bias, b_query, b_out, b_down, b_up, b_keyval, pad]
-    )
-    pars = pars.astype(F32).reshape(8 + FF // D, D)
     scratch = scratch_of(z)
     names = list(scratch)
-    n_in, n_out = 10, 9
+    n_in, n_out = 18, 9
 
     def call(*refs):
         m = Names()
@@ -962,22 +967,13 @@
             shape((z.CW, z.DW // 2), F32),
             shape((z.R, z.C4), F32),
             shape((z.R, z.C4), F32),
-            shape((z.R, z.KR), F32),
+            shape((z.KR, z.R), F32),
             shape((8, D), F32),
             shape((24, 128), F32),
         ],
-        in_specs=[
-            anywhere,
-            anywhere,
-            pl.BlockSpec(memory_space=pltpu.SMEM),
-            vmem,
-            anywhere,
-            anywhere,
-            anywhere,
-            anywhere,
-            anywhere,
-            anywhere,
-        ],
+        in_specs=[anywhere, anywhere, pl.BlockSpec(memory_space=pltpu.SMEM)]
+        + [anywhere] * 6
+        + [vmem] * 9,
         out_specs=[anywhere, anywhere] + [vmem] * 7,
         scratch_shapes=list(scratch.values()),
         compiler_params=pltpu.CompilerParams(
@@ -987,33 +983,71 @@
         hidden_in.reshape(z.ROWS, D),
         out_grad.reshape(z.ROWS, D),
         lengths,
-        pars,
         w_query,
         w_keyval,
         w_out,
         w_up,
         w_down,
         jnp.asarray(rotary_tables(z.LEN)),
+        ln1_gain,
+        ln1_bias,
+        ln2_gain,
+        ln2_bias,
+        b_query,
+        b_out,
+        b_down,
+        b_up,
+        b_keyval,
     )
-    flat = sw.reshape(-1)
-    b_down_grad = sv[6]
+    wide = (lo, gi, up, wo, wq)
+
+    def hand_over(*refs):
+        n = len(wide)
+        sources, (dn, wkv, sv, sw) = refs[:n], refs[n : n + 4]
+        targets, rest = refs[n + 4 : 2 * n + 4], refs[2 * n + 4 : 2 * n + 15]
+        held, came, left = refs[2 * n + 15 : 3 * n + 15], refs[-2], refs[-1]
+        copies = [
+            (
+                pltpu.make_async_copy(a, b, came.at[k]),
+                pltpu.make_async_copy(b, c, left.at[k]),
+            )
+            for k, (a, b, c) in enumerate(zip(sources, held, targets))
+        ]
+        for copy, _ in copies:
+            copy.start()
+        o_dn, o_wkv, gain_one, shift_one, gain_two, shift_two, bq, bkv, bo, bup, bd = rest
+        for at, ref in enumerate((gain_one, shift_one, bq)):
+            parts = [sw[k : k + 1, :] for k in range(at * (D // 128), (at + 1) * (D // 128))]
+            ref[...] = jnp.concatenate(parts, axis=1).reshape(D)
+        bkv[...] = sw[18:19, :].reshape(PAIR)
+        gain_two[...] = sv[4:5, :].reshape(D)
+        shift_two[...] = sv[5:6, :].reshape(D)
+        bo[...] = sv[6:7, :].reshape(D)
+        bd[...] = sv[6:7, :].reshape(D)
+        parts = [sv[k : k + 1, :] for k in range(FF // D)]
+        bup[...] = jnp.concatenate(parts, axis=1).reshape(FF)
+        o_dn[...] = jnp.transpose(dn[...])
+        o_wkv[...] = wkv[...]
+        for copy, out in copies:
+            copy.wait()
+            out.start()
+        for _, out in copies:
+            out.wait()
+
+    lo, gi, up, wo, wq, dn, wkv, g1, s1, g2, s2, bq, bkv, bo, bup, bd = pl.pallas_call(
+        hand_over,
+        out_shape=[shape(v.shape, v.dtype) for v in wide]
+        + [shape(dn.shape[::-1], F32), shape(wkv.shape, F32)]
+        + [shape((n,), F32) for n in (D, D, D, D, D, PAIR, D, FF, D)],
+        in_specs=[anywhere] * 5 + [vmem] * 4,
+        out_specs=[anywhere] * 5 + [vmem] * 11,
+        scratch_shapes=[pltpu.VMEM(v.shape, v.dtype) for v in wide]
+        + [pltpu.SemaphoreType.DMA((5,)), pltpu.SemaphoreType.DMA((5,))],
+    )(*wide, dn, wkv, sv, sw)
     return (
         lo.reshape(hidden_in.shape),
         gi.reshape(hidden_in.shape),
-        flat[0:D],
-        flat[D : 2 * D],
-        sv[4],
-        sv[5],
-        wq,
-        flat[2 * D : 3 * D],
-        wkv,
-        flat[3 * D : 3 * D + 2 * HEAD],
-        wo,
-        b_down_grad,
-        up,
-        sv[: FF // D].reshape(FF),
-        dn,
-        b_down_grad,
+        g1, s1, g2, s2, wq, bq, wkv.T, bkv, wo, bo, up, bup, dn.T, bd,
     )
 
 

time: 151 us -> 132 us (0.87)
  local copies, waits for them, and re-layouts: 23.2 us -> 0 us
  Pallas kernels: 126 us -> 131 us
    unnamed x27 -> x0, local copies, waits for them, and re-layouts: 16.8 us -> none
    slice x4 -> x0, local copies, waits for them, and re-layouts: 4.91 us -> none  [the longest x1 1.48 us: body(): b_down_grad = sv[6]]
    pallas_call x0 -> x1, Pallas kernels: none -> 4.83 us  [body(): pl.pallas_call(hand_over, out_shape=[shape(v.shape, v.dtype) for v in wid...]
where the time goes in v3:
time: 132 us
  Pallas kernels  131 us (99%)
    pallas_call x1, Pallas kernels, body(): pl.pallas_call(call, out_shape=[shape((z.ROWS, D), BF), shape((z.ROWS, D)...  126 us
    pallas_call x1, Pallas kernels, body(): pl.pallas_call(hand_over, out_shape=[shape(v.shape, v.dtype) for v in wid...  4.83 us

profile of v3, /device:TPU:0, one launch (start us, length us, event | category | flops | bytes accessed | tf_op | source)
XLA Modules:
  0.0 131.7 jit_solution(15143487084023321520)
XLA Ops:
  0.7 126.0 %shard_map.297 = (bf16[512,768]{1,0:T(8,128)(2,1)}, f32[512,768]{1,0:T(8,128)}, f32[96,768]{1,0:T(8,128)}, f32[384,192]{1,0:T(8,128)}, f32[96,192]{1,0:T(8,128)}...) custom-call(bf16[512,768]{1,0:T(8,128)(2,1)} %bitcast.6, ...), custom_call_target="tpu_custom_call" | custom-call | tf_op jit(solution)/shard_map/pallas_call | solution.py:961
  126.6 4.8 %shard_map.298 = (bf16[512,768]{1,0:T(8,128)(2,1)}, f32[512,768]{1,0:T(8,128)}, f32[96,768]{1,0:T(8,128)}, f32[96,192]{1,0:T(8,128)}, f32[96,192]{1,0:T(8,128)},...) custom-call(bf16[512,768]{1,0:T(8,128)(2,1)} %get-tuple-element.41.r, ...), custom_call_target="tpu_custom_call" | custom-call | tf_op jit(solution)/shard_map/pallas_call | solution.py:1037

commit v4 on v3

--- a/solution.py
+++ b/solution.py
@@ -10,6 +10,15 @@
 
 HEAD = 64
 ROT = 16
+DK_PLAN = {
+    (0, 1): -2, (0, 2): -1, (0, 3): 1, (1, 1): -1, (1, 2): 2, (1, 3): 4,
+    (2, 1): 1, (2, 2): 3, (2, 3): 5, (3, 1): 3, (3, 2): 5, (3, 3): 6,
+}
+PLAN = {
+    "y0": 0, "y1": 0, "y2": 1, "y3": 2, "d00": 2, "d01": 4, "d10": 5, "dn0": 5, "cross": 2,
+    "e10": 1, "e11": 3, "e00": 5, "ey": 7, "dn1": 7,
+    "u01": 0, "u21": 1, "u02": 2, "u22": 3, "u11": 4, "u12": 5, "u03": 4, "u23": 5, "u13": 7,
+}
 PAIR = 2 * HEAD
 MESH = pl.DeviceIdType.MESH
 BF = jnp.bfloat16
@@ -197,7 +206,7 @@
         self.ROWS, self.LEN, self.HF = SL * SPAN, NS * SPAN, FF // 2
         self.QN = NJ // 2
         self.R, self.W = D // NS, FF // NJ
-        self.CH = NS // 2
+        self.CH = self.G = NS // 2
         self.CW = self.HF // self.CH
         self.CPP = self.W // self.CW
         self.FRH, self.DW = self.CW // 2, D // self.QN
@@ -240,23 +249,25 @@
         dks=vm((z.SL, z.NS, PAIR, z.SPAN), BF),
         dkr=vm((z.SL, z.NS - 1, PAIR, z.SPAN), BF),
         up=vm((z.CH, z.NS, z.R, z.CW), BF),
-        upr=vm((z.CH, z.NS - 1, z.R, z.CW), BF),
-        upf=vm((z.CPP, z.QN, z.R, z.CW), BF),
+        upr=vm((z.CH if z.CPP == 1 else z.CH // 2 + 1, z.NS - 1, z.R, z.CW), BF),
+        upf=vm((z.QN, z.R, z.CW), BF),
+        upy=vm((z.QN if z.CPP > 1 else 1, z.NS if z.CPP > 1 else 1, z.R, z.CW), BF),
         dn=vm((z.CH, 2, z.QN, z.FRH, z.DW), BF),
-        dnr=vm((z.CH, 2, z.QN - 1, z.FRH, z.DW), BF),
-        dnr2=vm((2 * z.CH - 2, z.FRH, z.DW), BF),
+        dnr=vm((z.CH + 1, z.QN - 1, z.FRH, z.DW), BF),
+        dnr2=vm((z.CH - 1, z.FRH, z.DW), BF),
+        dnr3=vm((z.CH - 1, z.QN, z.FRH, z.DW), BF),
         dnm=vm((4, z.FRH, z.DW // 2), BF),
         dnf=vm((2, 2, z.FRH, z.DW // 2), BF),
         wo=vm((2, z.NS, z.R2, d), BF),
-        wor=vm((2, z.NS - 1, z.R2, d), BF),
+        wor=vm((2, z.G, z.R2, d), BF),
+        woq=vm((2, z.G, z.R2, d), BF),
         wos=vm((2, z.NJ, z.R2, z.C4), BF),
-        wof=vm((2, z.NJ, z.R2, z.C4), BF),
-        wox=vm((2, 2, z.R2, z.C4), F32),
-        woy=vm((2, 2, z.R2, z.C4), BF),
+        wof=vm((2 * z.NJ, z.R2, z.C4), BF),
         gq=vm((2, 2 * z.NS, z.R2, d // 2), BF),
-        gqr=vm((2, 2 * z.NS - 1, z.R2, d // 2), BF),
-        gqs=vm((2, z.QN, z.R2, z.C4), BF),
-        gqf=vm((z.NJ, z.R2, z.C4), BF),
+        gqr=vm((2, z.NS, z.R2, d // 2), BF),
+        gqq=vm((2, z.G, 2, z.R2, d // 2), BF),
+        gqs=vm((2, 2 * z.QN, z.R2, z.C4), BF),
+        gqf=vm((2 * z.NJ, z.R2, z.C4), BF),
         kgs=vm((z.NJ, z.KR, d), BF),
         kgf=vm((z.NJ, z.KR, d), BF),
         kg2=vm((z.NS, z.KR, z.R), BF),
@@ -362,19 +373,40 @@
     pl.semaphore_wait(barrier, len(near))
     got_m.start()
     got_g.start()
-    gather = []
-    for d in range(1, NS):
-        up_to = lax.rem(s + d, NS)
-        copy = links.copy(m.kv.at[:, s], m.kv.at[:, s], seq_device(up_to))
-        sends = s + d < NS
-        gets = s - d >= 0
-        gather.append((copy, sends, gets))
+    inner = lax.rem(s, 2)
+    outer = lax.div(s, 2)
+    NO = NS // 2
+    far, near_by = {}, {}
+    for d in range(NO):
+        gets = outer - d >= 0
+        if d:
+            sends = outer + d < NO
+            there = seq_device(lax.rem(s + 2 * d, NS))
+            far[d] = (links.copy(m.kv.at[:, s], m.kv.at[:, s], there), gets)
+
+            @pl.when(sends)
+            def _(d=d):
+                far[d][0].start()
+
+            links.waits.append((sends, far[d][0]))
+            sends = gets
+        else:
+            sends, gets = inner == 0, inner == 1
+        block = lax.rem(s - 2 * d + NS, NS)
+        copy = links.copy(m.kv.at[:, block], m.kv.at[:, block], seq_device(flip(s, 0)))
+        near_by[d] = (copy, sends, gets)
+        links.waits.append((sends, copy))
+
+    def pass_on(d):
+        copy, sends, _ = near_by[d]
 
         @pl.when(sends)
-        def _(copy=copy):
+        def _():
+            if d:
+                far[d][0].wait_recv()
             copy.start()
 
-        links.waits.append((sends, copy))
+    pass_on(0)
 
     load_wq.wait()
     load_wout.wait()
@@ -399,23 +431,60 @@
     turned_bits = low_bits[1:] + low_bits[:1]
     seq_stage = lambda b: (bit_of(s, b), (flip(s, b), j))
     slot_stage = lambda b: (bit_of(j, b), (s, flip(j, b)))
+    low_s = lax.rem(s, z.G)
+    slot_stages = [slot_stage(b) for b in range(BJ - 1, 0, -1)]
     dn_first = [
-        [
-            Halving(
-                links,
-                m.dn.at[k, p],
-                [slot_stage(b) for b in range(BJ - 1, 0, -1)],
-                m.dnr.at[k, p],
-            )
-            for p in range(2)
-        ]
-        for k in range(z.CH)
+        Halving(links, m.dn.at[k, 0], slot_stages, m.dnr.at[k]) for k in range(z.CH)
     ]
+    dn_other = {}
+    at = 0
+    for l in range(BS - 2, -1, -1):
+        for n in range(2**l):
+            keep = lax.div(low_s, 2**l) * 2**l + n
+            give = keep + (1 - 2 * bit_of(s, l)) * 2**l
+            copy = links.copy(m.dn.at[give, 1], m.dnr3.at[at], (flip(s, l), j))
+            dn_other[l, n] = (copy, keep, at)
+            at += 1
+    dn_second = Halving(links, m.dn.at[low_s, 1], slot_stages, m.dnr.at[z.CH])
+
+    def other_start(l, n):
+        dn_other[l, n][0].start()
+        links.waits.append(dn_other[l, n][0])
+
+    def other_finish(l, n):
+        copy, keep, at = dn_other[l, n]
+        copy.wait_recv()
+        for q in range(QN):
+            m.dn[keep, 1, q] = m.dn[keep, 1, q] + m.dnr3[at, q]
+
     up_order = [(low_bits if k % 2 == 0 else turned_bits) + [BS - 1] for k in range(z.CH)]
-    ups = [
-        Halving(links, m.up.at[k], [seq_stage(b) for b in up_order[k]], m.upr.at[k])
-        for k in range(z.CH)
-    ]
+    crossing = [k for k in range(z.CH) if k % z.CPP == 1]
+    staying = [k for k in range(z.CH) if k not in crossing]
+    ups = {
+        k: Halving(links, m.up.at[k], [seq_stage(b) for b in up_order[k]], m.upr.at[n])
+        for n, k in enumerate(staying)
+    }
+    if crossing:
+        stages = [seq_stage(b) for b in up_order[1]]
+        ups[1] = Halving(links, m.upy.at[0], stages, m.upr.at[len(staying)])
+    upy_arrivals = links.take(QN)
+    crossings = {}
+    for k in crossing:
+        target = c * QN + (k * CW) // z.W
+        crossings[k] = links.unless(
+            target == j, m.up.at[k], m.upy.at[rank], (s, target), upy_arrivals + rank
+        )
+
+    def crossed():
+        for n in range(QN):
+            links.arrived(m.upy.at[n], upy_arrivals + n)
+
+        def add(i, _):
+            m.upy[0, i] = m.upy[0, i] + m.upy[1, i]
+            return 0
+
+        lax.fori_loop(0, NS, add, 0)
+        ups[1].start(0)
 
     RB = 256
 
@@ -449,11 +518,16 @@
         for p in range(2):
             for q in range(QN):
                 m.dn[k, p, q] = part[p * z.FRH : (p + 1) * z.FRH, q * z.DW : (q + 1) * z.DW]
-            dn_first[k][p].start(0)
+        dn_first[k].start(0)
+        if 2 * k >= z.CH:
+            other_start(BS - 2, k - z.CH // 2)
         part = dot(m.mlp2[...], m.dup[:, cols], 0, 0).astype(BF)
         for n in range(NS):
-            m.up[k, placed(n, up_order[k])] = part[n * R : (n + 1) * R, :]
-        ups[k].start(0)
+            m.up[k, placed(n, up_order[1 if k in crossing else k])] = part[n * R : (n + 1) * R, :]
+        if k in crossing:
+            crossings[k]()
+        else:
+            ups[k].start(0)
 
     halfway = ROWS // RB
     totals = []
@@ -464,74 +538,79 @@
             got_g.wait()
         totals.append(total + feed(k, halfway, 2 * halfway))
         feed_grads(k)
+        for d in range(1, NO):
+            if (k == d if NO == 4 else k == z.CH - 1):
+                pass_on(d)
     total = jnp.concatenate(totals, axis=1)
     for q in range(z.FF // D):
         piece = total[:, (q * D) % HF : (q * D) % HF + D]
         m.sv[0, q : q + 1, :] = jnp.where(c == (q * D) // HF, piece, 0.0)
 
     kept = rank
-    dn_levels, at = [], 0
+    dn_levels, at = {}, 0
     for l in range(BS - 1):
-        level = []
         for n in range(z.CH >> (l + 1)):
             base = n * 2 ** (l + 1) + lax.rem(s, 2**l)
             mine = bit_of(s, l)
             keep = base + mine * 2**l
             give = base + (1 - mine) * 2**l
-            for p in range(2):
-                copy = links.copy(m.dn.at[give, p, kept], m.dnr2.at[at], (flip(s, l), j))
-                level.append((copy, keep, p, at, n))
-                at += 1
-        dn_levels.append(level)
+            copy = links.copy(m.dn.at[give, 0, kept], m.dnr2.at[at], (flip(s, l), j))
+            dn_levels[l, n] = (copy, keep, at)
+            at += 1
 
     def dn_start(l, n):
-        for copy, keep, p, at, group in dn_levels[l]:
-            if group == n:
-                copy.start()
-                links.waits.append(copy)
+        dn_levels[l, n][0].start()
+        links.waits.append(dn_levels[l, n][0])
 
     def dn_finish(l, n):
-        for copy, keep, p, at, group in dn_levels[l]:
-            if group == n:
-                copy.wait_recv()
-                m.dn[keep, p, kept] = m.dn[keep, p, kept] + m.dnr2[at]
+        copy, keep, at = dn_levels[l, n]
+        copy.wait_recv()
+        m.dn[keep, 0, kept] = m.dn[keep, 0, kept] + m.dnr2[at]
 
     dn_arrivals = links.take(4)
 
-    def dn_last():
-        mine = lax.rem(s, z.CH)
-        for p in range(2):
-            part = m.dn[mine, p, kept]
-            for h in range(2):
-                m.dnm[2 * p + h] = part[:, h * (z.DW // 2) : (h + 1) * (z.DW // 2)]
-                links.unless(
-                    jnp.logical_and(ts == c, c == h),
-                    m.dnm.at[2 * p + h],
-                    m.dnf.at[p, ts],
-                    (put(s, BS - 1, c), put(j, 0, h)),
-                    dn_arrivals + 2 * p + ts,
-                )()
-
-    up_arrivals = links.take(z.CPP * QN)
+    dn_ends = [
+        [
+            links.unless(
+                jnp.logical_and(ts == c, c == h),
+                m.dnm.at[2 * p + h],
+                m.dnf.at[p, ts],
+                (put(s, BS - 1, c), put(j, 0, h)),
+                dn_arrivals + 2 * p + ts,
+            )
+            for h in range(2)
+        ]
+        for p in range(2)
+    ]
+
+    def dn_last(p):
+        part = m.dn[low_s, p, kept]
+        for h in range(2):
+            m.dnm[2 * p + h] = part[:, h * (z.DW // 2) : (h + 1) * (z.DW // 2)]
+            dn_ends[p][h]()
+
+    up_arrivals = links.take(QN)
 
     def up_end(k):
-        piece, n = (k * CW) // z.W, k % z.CPP
-        target = c * QN + piece
+        target = c * QN + (k * CW) // z.W
         return links.unless(
-            target == j,
-            m.up.at[k, ups[k].end],
-            m.upf.at[n, rank],
-            (s, target),
-            up_arrivals + n * QN + rank,
+            target == j, m.up.at[k, ups[k].end], m.upf.at[rank], (s, target), up_arrivals + rank
         )
 
-    up_last = [up_end(k) for k in range(z.CH)]
-
+    up_last = {k: up_end(k) for k in range(z.CH) if k not in crossing}
+
+    def group_device(n):
+        return (ts * z.G + n, j)
+
+    dk_bits = [
+        (low_bits if i % 2 == 0 else turned_bits) + [BS - 1] for i in range(SL)
+    ]
     dkvs = [
-        Halving(links, m.dks.at[i], [seq_stage(b) for b in range(BS)], m.dkr.at[i])
+        Halving(links, m.dks.at[i], [seq_stage(b) for b in dk_bits[i]], m.dkr.at[i])
         for i in range(SL)
     ]
-    pos = [placed(n, list(range(BS))) for n in range(NS)]
+    dk_place = [[placed(n, dk_bits[i]) for n in range(NS)] for i in range(2)]
+
     coef = scale * math.log2(math.e)
     key_spot = lax.broadcasted_iota(jnp.int32, (SPAN, LEN), 1)
     row_spot = s * SPAN + lax.broadcasted_iota(jnp.int32, (SPAN, LEN), 0)
@@ -605,8 +684,8 @@
                 for step in steps:
                     step()
 
-    kv_in = []
-    for copy, sends, gets in gather:
+    for d in range(NO):
+        copy, _, gets = near_by[d]
 
         @pl.when(gets)
         def _(copy=copy):
@@ -615,15 +694,11 @@
     def up_step(k, n):
         return lambda: ups[k].step(n)
 
-    def dn_y(k):
-        def go():
-            for p in range(2):
-                for n in range(BJ - 1):
-                    dn_first[k][p].finish(n)
-                    if n + 1 < BJ - 1:
-                        dn_first[k][p].start(n + 1)
-
-        return go
+    def slots_done(pipe):
+        for n in range(BJ - 1):
+            pipe.finish(n)
+            if n + 1 < BJ - 1:
+                pipe.start(n + 1)
 
     early = {n: [] for n in range(SL)}
     late = {n: [] for n in range(SL)}
@@ -633,21 +708,37 @@
     def at_point(n, step):
         plan[min(n, 2 * SL)].append(step)
 
+    small = BS == 3 and z.CPP == 2
+    order = PLAN if small else {}
+
+    def at(name, step):
+        plan[order.get(name, 2 * SL)].append(step)
+
     for k in range(z.CH):
-        for n in range(1, BS + 1):
-            at_point(k // 2 + 2 * (n - 1) if BS == 3 else 2 * SL, up_step(k, n))
-        at_point(k // 2 + 2 * BS - 2 if BS == 3 else 2 * SL, lambda k=k: up_last[k]())
-    for k in range(z.CH):
-        at_point(1 + k if BS == 3 else 2 * SL, dn_y(k))
+        at(f"y{k}", lambda k=k: slots_done(dn_first[k]))
         if k % 2 == 1:
-            at_point(1 + k if BS == 3 else 2 * SL, lambda k=k: dn_start(0, k // 2))
+            at(f"y{k}", lambda k=k: dn_start(0, k // 2))
     for l in range(BS - 1):
         for n in range(z.CH >> (l + 1)):
-            point = (5 + 2 * n if l == 0 else 8) if BS == 3 else 2 * SL
-            at_point(point, lambda l=l, n=n: dn_finish(l, n))
+            at(f"d{l}{n}", lambda l=l, n=n: dn_finish(l, n))
             if l + 1 < BS - 1 and n % 2 == 1:
-                at_point(point, lambda l=l, n=n: dn_start(l + 1, n // 2))
-    at_point(2 * SL, dn_last)
+                at(f"d{l}{n}", lambda l=l, n=n: dn_start(l + 1, n // 2))
+    at("dn0", lambda: dn_last(0))
+    for l in range(BS - 2, -1, -1):
+        for n in range(2**l):
+            at(f"e{l}{n}", lambda l=l, n=n: other_finish(l, n))
+            if l > 0 and n >= 2 ** (l - 1):
+                at(f"e{l}{n}", lambda l=l, n=n: other_start(l - 1, n - 2 ** (l - 1)))
+    at("e00", lambda: dn_second.start(0))
+    at("ey", lambda: slots_done(dn_second))
+    at("dn1", lambda: dn_last(1))
+    if crossing:
+        at("cross", crossed)
+    for k in ups:
+        for n in range(1, BS + 1):
+            at(f"u{k}{n}", up_step(k, n))
+        if k not in crossing:
+            at(f"u{k}{BS}", up_last[k])
 
     def early_body(i, _):
         m.dkt[i] = attend(0, i).astype(m.dkt.dtype)
@@ -656,96 +747,120 @@
 
     lax.fori_loop(0, SL, early_body, 0)
 
-    wo_order = [turned_bits, low_bits]
-    wo_pipes = [
-        Halving(
+    wo_core = [Halving(links, m.wo.at[hg], [slot_stage(0)], m.wor.at[hg]) for hg in range(2)]
+    gq_core = [Halving(links, m.gq.at[hg], [slot_stage(0)], m.gqr.at[hg]) for hg in range(2)]
+    wo_group = [
+        Direct(
             links,
-            m.wo.at[hg],
-            [slot_stage(0)] + [seq_stage(b) for b in wo_order[hg]],
-            m.wor.at[hg],
+            z.G,
+            low_s,
+            group_device,
+            lambda n, hg=hg: m.wo.at[hg, c * z.G + n],
+            m.woq.at[hg],
         )
         for hg in range(2)
     ]
-    gq_order = [low_bits + [BS - 1], turned_bits + [BS - 1]]
-    gq_pipes = [
-        Halving(
+    gq_group = [
+        Direct(
             links,
-            m.gq.at[hg],
-            [slot_stage(0)] + [seq_stage(b) for b in gq_order[hg]],
-            m.gqr.at[hg],
+            z.G,
+            low_s,
+            group_device,
+            lambda n, hg=hg: m.gq.at[hg, pl.ds(c * NS + 2 * n, 2)],
+            m.gqq.at[hg],
         )
         for hg in range(2)
     ]
-    gq_arrivals = links.take(NJ)
+    wo_arrivals = links.take(2 * NJ)
+    gq_arrivals = links.take(2 * NJ)
+    me = ts * NJ + j
+    wo_ends = [
+        [
+            links.unless(
+                jnp.logical_and(ts == hg, j == n),
+                m.wos.at[hg, n],
+                m.wof.at[me],
+                (hg * z.G + low_s, n),
+                wo_arrivals + me,
+            )
+            for n in range(NJ)
+        ]
+        for hg in range(2)
+    ]
+    gq_ends = [
+        [
+            links.unless(
+                jnp.logical_and(ts == t, j == hg * QN + n),
+                m.gqs.at[hg, t * QN + n],
+                m.gqf.at[me],
+                (t * z.G + low_s, hg * QN + n),
+                gq_arrivals + me,
+            )
+            for t in range(2)
+            for n in range(QN)
+        ]
+        for hg in range(2)
+    ]
 
     def project(hg):
         cols = slice(hg * (D // 2), (hg + 1) * (D // 2))
         part = dot(m.att[:, cols], m.g2[0:ROWS, :], 0, 0).astype(BF)
-        for n in range(NS // 2):
+        for n in range(z.G):
             for r in range(2):
                 at = n * R + r * R2
-                m.wo[hg, r * (NS // 2) + placed(n, wo_order[hg])] = part[at : at + R2, :]
-        wo_pipes[hg].start(0)
+                m.wo[hg, r * z.G + n] = part[at : at + R2, :]
+        wo_core[hg].start(0)
         part = dot(m.ain[...], m.dq[:, cols], 0, 0).astype(BF)
         for n in range(NS):
             for r in range(2):
                 at = n * R + r * R2
-                m.gq[hg, r * NS + placed(n, gq_order[hg])] = part[at : at + R2, :]
-        gq_pipes[hg].start(0)
-
-    wo_direct = [
-        Direct(links, NJ, j, slot_device, lambda n, hg=hg: m.wos.at[hg, n], m.wof.at[hg])
-        for hg in range(2)
-    ]
-
-    def wo_last(hg):
-        part = m.wo[hg, wo_pipes[hg].end]
+                m.gq[hg, r * NS + (n % z.G) * 2 + n // z.G] = part[at : at + R2, :]
+        gq_core[hg].start(0)
+
+    def project_group(hg):
+        wo_core[hg].finish(0)
+        wo_group[hg].start()
+        gq_core[hg].finish(0)
+        gq_group[hg].start()
+
+    def project_last(hg):
+        wo_group[hg].finish()
+        total = m.wo[hg, c * z.G + low_s].astype(F32)
+        for d in range(1, z.G):
+            total = total + m.woq[hg, lax.rem(low_s + d, z.G)].astype(F32)
+        total = total.astype(BF)
         for n in range(NJ):
-            m.wos[hg, n] = part[:, n * C4 : (n + 1) * C4]
-        m.wof[hg, j] = m.wos[hg, j]
-        wo_direct[hg].start()
-
-    def wo_sum(hg):
-        wo_direct[hg].finish()
-        for r in range(2):
-            total = m.wof[hg, r].astype(F32)
-            for n in range(1, QN):
-                total = total + m.wof[hg, 2 * n + r].astype(F32)
-            m.wox[hg, r] = total
-
-    def gq_last(hg):
-        part = m.gq[hg, gq_pipes[hg].end]
-        for n in range(QN):
-            m.gqs[hg, n] = part[:, n * C4 : (n + 1) * C4]
-            target = hg * QN + n
-            links.unless(
-                target == j, m.gqs.at[hg, n], m.gqf.at[j], (s, target), gq_arrivals + j
-            )()
+            m.wos[hg, n] = total[:, n * C4 : (n + 1) * C4]
+            wo_ends[hg][n]()
+        gq_group[hg].finish()
+        for t in range(2):
+            total = m.gq[hg, c * NS + 2 * low_s + t].astype(F32)
+            for d in range(1, z.G):
+                total = total + m.gqq[hg, lax.rem(low_s + d, z.G), t].astype(F32)
+            total = total.astype(BF)
+            for n in range(QN):
+                m.gqs[hg, t * QN + n] = total[:, n * C4 : (n + 1) * C4]
+                gq_ends[hg][t * QN + n]()
 
     project(0)
-    small = BS == 3
-    if small:
-        late[0] += [lambda: wo_pipes[0].step(1), lambda: gq_pipes[0].step(1)]
-        late[2] += [lambda: wo_pipes[0].step(2), lambda: gq_pipes[0].step(2)]
-        late[3] += [lambda: wo_pipes[0].step(3), lambda: gq_pipes[0].step(3)]
-        late[3] += [lambda: wo_last(0)]
-        tail += [lambda: gq_pipes[0].step(4), lambda: gq_last(0)]
-    else:
-        for n in range(1, BS + 1):
-            tail += [lambda n=n: wo_pipes[0].step(n)]
-        tail += [lambda: wo_last(0)]
-        for n in range(1, BS + 2):
-            tail += [lambda n=n: gq_pipes[0].step(n)]
-        tail += [lambda: gq_last(0)]
+    late[0] += [lambda: project_group(0)]
+    late[2] += [lambda: project_last(0)]
+    marks = {n: [] for n in range(1, 7)}
     for i in range(SL):
         for n in range(1, BS + 1):
-            if i + n < SL:
-                late[i + n] += [lambda i=i, n=n: dkvs[i].step(n)]
+            where = DK_PLAN[i, n] if small and SL == 4 else 6
+            step = lambda i=i, n=n: dkvs[i].step(n)
+            (late[where + 4] if where < 0 else marks[where]).append(step)
+
+    def mark(n):
+        for step in marks[n]:
+            step()
 
     def late_body(i, _):
         total = (m.dkt[i] + attend(1, i)).astype(BF)
         for n in range(NS):
-            m.dks[i, pos[n]] = total[:, n * SPAN : (n + 1) * SPAN]
+            place = jnp.where(lax.rem(i, 2) == 0, dk_place[0][n], dk_place[1][n])
+            m.dks[i, place] = total[:, n * SPAN : (n + 1) * SPAN]
         for n in range(SL):
 
             @pl.when(i == n)
@@ -757,45 +872,32 @@
 
     lax.fori_loop(0, SL, late_body, 0)
 
-    left = []
-    for i in range(SL):
-        for n in range(1, BS + 1):
-            if i + n >= SL:
-                left.append((i + n - SL, lambda i=i, n=n: dkvs[i].step(n)))
-
-    def dkv_round(r):
-        for at, step in left:
-            if at == r:
-                step()
-
     project(1)
-    dkv_round(0)
-    for step in tail:
-        step()
     for k in range(halfway):
         rows = slice(ROWS + k * RB, ROWS + (k + 1) * RB)
         here = slice(k * RB, (k + 1) * RB)
         msend[here, :] = dot(m.act[rows, :], m.wdn[...]).astype(BF)
+    project_group(1)
+    mark(1)
     for k in range(halfway):
         rows = slice(ROWS + k * RB, ROWS + (k + 1) * RB)
         here = slice(k * RB, (k + 1) * RB)
         dsend[here, :] = dot(m.dup[rows, :], m.wup[...], 1, 1).astype(BF)
     got_out = links.start(msend, mrecv, buddy)
     got_back = links.start(dsend, drecv, buddy)
-    wo_pipes[1].step(1)
-    gq_pipes[1].step(1)
-    dkv_round(1)
+    mark(2)
+    for step in tail:
+        step()
     for k in range(halfway):
         here = slice(k * RB, (k + 1) * RB)
         m.own_mlp[here, :] = dot(m.act[here, :], m.wdn[...]) + dot(m.att[here, :], m.wout[...])
+    mark(3)
+    for k in range(halfway):
+        here = slice(k * RB, (k + 1) * RB)
         m.own_d[here, :] = dot(m.dup[here, :], m.wup[...], 1, 1).astype(m.own_d.dtype)
+    mark(4)
     got_out.wait_recv()
     got_back.wait_recv()
-    dkv_round(2)
-    for step in range(2, BS + 1):
-        wo_pipes[1].step(step)
-        gq_pipes[1].step(step)
-    wo_last(1)
 
     def normed(rows):
         v = m.x[rows, :].astype(F32)
@@ -828,10 +930,16 @@
     sv_two = Direct(links, NS, s, seq_device, lambda n: m.sv.at[1], m.svb)
     m.sva[j] = m.sv[0]
     sv_one.start()
-
-    dkv_round(3)
-    gq_pipes[1].step(BS + 1)
-    gq_last(1)
+    mark(5)
+
+    bq = jnp.zeros((1, D), F32)
+    for i in range(SL):
+        rows = slice(i * SPAN, (i + 1) * SPAN)
+        dq = m.dq[rows, :]
+        bq = bq + jnp.sum(dq.astype(F32), axis=0, keepdims=True)
+        m.own_mlp[rows, :] = dot(dq, m.wq[...], 1, 1)
+    project_last(1)
+    mark(6)
 
     bkv = jnp.zeros((1, PAIR), F32)
     for i in range(SL):
@@ -850,22 +958,13 @@
 
     gain_one = jnp.zeros((1, D), F32)
     shift_one = jnp.zeros((1, D), F32)
-    bq = jnp.zeros((1, D), F32)
     for i in range(SL):
         rows = slice(i * SPAN, (i + 1) * SPAN)
-        dq = m.dq[rows, :]
-        bq = bq + jnp.sum(dq.astype(F32), axis=0, keepdims=True)
-        d_in = dot(dq, m.wq[...], 1, 1) + dot(m.kvs[rows, :], m.wkv[...], 1, 1)
-        unit, inv = normed(rows)
+        d_in = m.own_mlp[rows, :] + dot(m.kvs[rows, :], m.wkv[...], 1, 1)
+        unit, _ = normed(rows)
         gain_one = gain_one + jnp.sum(d_in * unit, axis=0, keepdims=True)
         shift_one = shift_one + jnp.sum(d_in, axis=0, keepdims=True)
-        d_unit = d_in * pars[0:1, :] + m.own_d[rows, :]
-        along = jnp.mean(d_unit * unit, axis=-1, keepdims=True)
-        d_unit = d_unit - jnp.mean(d_unit, axis=-1, keepdims=True) - unit * along
-        m.own_mlp[rows, :] = m.g2[rows, :].astype(F32) + d_unit * inv
-    copy = pltpu.make_async_copy(m.own_mlp, o_gi, m.lsem.at[9])
-    copy.start()
-    out_copies.append(copy)
+        m.own_mlp[rows, :] = d_in
     m.sw[0] = jnp.zeros((24, 128), F32)
     for n in range(D // 128):
         cols = slice(n * 128, (n + 1) * 128)
@@ -877,6 +976,16 @@
     sw_two = Direct(links, NS, s, seq_device, lambda n: m.sw.at[1], m.swb)
     m.swa[j] = m.sw[0]
     sw_one.start()
+    for i in range(SL):
+        rows = slice(i * SPAN, (i + 1) * SPAN)
+        unit, inv = normed(rows)
+        d_unit = m.own_mlp[rows, :] * pars[0:1, :] + m.own_d[rows, :]
+        along = jnp.mean(d_unit * unit, axis=-1, keepdims=True)
+        d_unit = d_unit - jnp.mean(d_unit, axis=-1, keepdims=True) - unit * along
+        m.own_mlp[rows, :] = m.g2[rows, :].astype(F32) + d_unit * inv
+    copy = pltpu.make_async_copy(m.own_mlp, o_gi, m.lsem.at[9])
+    copy.start()
+    out_copies.append(copy)
 
     def summed(ref, size):
         total = ref[0].astype(F32)
@@ -899,30 +1008,24 @@
     m.swb[s] = m.sw[1]
     sw_two.start()
 
-    wo_sum(0)
-    wo_sum(1)
-    for r in range(2):
-        m.woy[0, r] = m.wox[1 - ts, r].astype(BF)
-    wo_end = links.start(m.woy.at[0], m.woy.at[1], (flip(s, BS - 1), j))
-
-    for n in range(z.CPP):
-        for r in range(QN):
-            links.arrived(m.upf.at[n, r], up_arrivals + n * QN + r)
-        o_up[:, n * CW : (n + 1) * CW] = summed(m.upf.at[n], QN)
+    if crossing:
+        o_up[:, CW:] = m.upy[0, ups[1].end].astype(F32)
+    for n in range(QN):
+        links.arrived(m.upf.at[n], up_arrivals + n)
+    o_up[:, 0:CW] = summed(m.upf, QN)
     for p in range(2):
         for t in range(2):
             links.arrived(m.dnf.at[p, t], dn_arrivals + 2 * p + t)
         o_dn[p * z.FRH : (p + 1) * z.FRH, :] = summed(m.dnf.at[p], 2)
-    for n in range(NJ):
+    for n in range(2 * NJ):
         links.arrived(m.gqf.at[n], gq_arrivals + n)
+        links.arrived(m.wof.at[n], wo_arrivals + n)
     for r in range(2):
-        total = m.gqf[r].astype(F32)
-        for n in range(1, QN):
-            total = total + m.gqf[2 * n + r].astype(F32)
-        o_wq[r * R2 : (r + 1) * R2, :] = total
-    wo_end.wait_recv()
-    for r in range(2):
-        o_wo[r * R2 : (r + 1) * R2, :] = m.wox[ts, r] + m.woy[1, r].astype(F32)
+        for out, ref in ((o_wq, m.gqf), (o_wo, m.wof)):
+            total = ref[r].astype(F32)
+            for n in range(1, NJ):
+                total = total + ref[2 * n + r].astype(F32)
+            out[r * R2 : (r + 1) * R2, :] = total
     sv_two.finish()
     o_sv[...] = summed(m.svb, NS)
     kg_two.finish()
@@ -977,7 +1080,7 @@
         out_specs=[anywhere, anywhere] + [vmem] * 7,
         scratch_shapes=list(scratch.values()),
         compiler_params=pltpu.CompilerParams(
-            collective_id=0, has_side_effects=True, vmem_limit_bytes=62 * 2**20
+            collective_id=0, has_side_effects=True, vmem_limit_bytes=63 * 2**20
         ),
     )(
         hidden_in.reshape(z.ROWS, D),

time: 132 us -> 120 us (0.909)
  Pallas kernels: 131 us -> 119 us
    pallas_call x1, Pallas kernels: 126 us -> 114 us  [body(): pl.pallas_call(call, out_shape=[shape((z.ROWS, D), BF), shape((z.ROWS, D)...]
where the time goes in v4:
time: 120 us
  Pallas kernels  119 us (99%)
    pallas_call x1, Pallas kernels, body(): pl.pallas_call(call, out_shape=[shape((z.ROWS, D), BF), shape((z.ROWS, D)...  114 us
    pallas_call x1, Pallas kernels, body(): pl.pallas_call(hand_over, out_shape=[shape(v.shape, v.dtype) for v in wid...  4.83 us

profile of v4, /device:TPU:0, one launch (start us, length us, event | category | flops | bytes accessed | tf_op | source)
XLA Modules:
  0.0 119.8 jit_solution(6747449250366133814)
XLA Ops:
  0.7 114.1 %shard_map.297 = (bf16[512,768]{1,0:T(8,128)(2,1)}, f32[512,768]{1,0:T(8,128)}, f32[96,768]{1,0:T(8,128)}, f32[384,192]{1,0:T(8,128)}, f32[96,192]{1,0:T(8,128)}...) custom-call(bf16[512,768]{1,0:T(8,128)(2,1)} %bitcast.6, ...), custom_call_target="tpu_custom_call" | custom-call | tf_op jit(solution)/shard_map/pallas_call | solution.py:1064
  114.8 4.8 %shard_map.298 = (bf16[512,768]{1,0:T(8,128)(2,1)}, f32[512,768]{1,0:T(8,128)}, f32[96,768]{1,0:T(8,128)}, f32[96,192]{1,0:T(8,128)}, f32[96,192]{1,0:T(8,128)},...) custom-call(bf16[512,768]{1,0:T(8,128)(2,1)} %get-tuple-element.41.r, ...), custom_call_target="tpu_custom_call" | custom-call | tf_op jit(solution)/shard_map/pallas_call | solution.py:1140

commit v5 on v4

--- a/solution.py
+++ b/solution.py
@@ -844,7 +844,7 @@
 
     project(0)
     late[0] += [lambda: project_group(0)]
-    late[2] += [lambda: project_last(0)]
+    late[1] += [lambda: project_last(0)]
     marks = {n: [] for n in range(1, 7)}
     for i in range(SL):
         for n in range(1, BS + 1):

time: 120 us -> 123 us (1.025)
  Pallas kernels: 119 us -> 122 us
    pallas_call x1, Pallas kernels: 114 us -> 117 us  [body(): pl.pallas_call(call, out_shape=[shape((z.ROWS, D), BF), shape((z.ROWS, D)...]
where the time goes in v5:
time: 123 us; the launch traced here: 122 us
  Pallas kernels  122 us (99%)
    pallas_call x1, Pallas kernels, body(): pl.pallas_call(call, out_shape=[shape((z.ROWS, D), BF), shape((z.ROWS, D)...  117 us
    pallas_call x1, Pallas kernels, body(): pl.pallas_call(hand_over, out_shape=[shape(v.shape, v.dtype) for v in wid...  4.83 us

profile of v5, /device:TPU:0, one launch (start us, length us, event | category | flops | bytes accessed | tf_op | source)
XLA Modules:
  0.0 122.5 jit_solution(13606280569856702195)
XLA Ops:
  0.7 116.8 %shard_map.297 = (bf16[512,768]{1,0:T(8,128)(2,1)}, f32[512,768]{1,0:T(8,128)}, f32[96,768]{1,0:T(8,128)}, f32[384,192]{1,0:T(8,128)}, f32[96,192]{1,0:T(8,128)}...) custom-call(bf16[512,768]{1,0:T(8,128)(2,1)} %bitcast.6, ...), custom_call_target="tpu_custom_call" | custom-call | tf_op jit(solution)/shard_map/pallas_call | solution.py:1064
  117.5 4.8 %shard_map.298 = (bf16[512,768]{1,0:T(8,128)(2,1)}, f32[512,768]{1,0:T(8,128)}, f32[96,768]{1,0:T(8,128)}, f32[96,192]{1,0:T(8,128)}, f32[96,192]{1,0:T(8,128)},...) custom-call(bf16[512,768]{1,0:T(8,128)(2,1)} %get-tuple-element.41.r, ...), custom_call_target="tpu_custom_call" | custom-call | tf_op jit(solution)/shard_map/pallas_call | solution.py:1140
